TPU v7x, 512 devices: a whole 4x4x16 slice. The times are simulated.
512 devices in a mesh: gy: 32 (over y_lo, z), gz: 16 (over y_hi, x, core).
Axes of the slice: x: 4, y: 4 (y_hi: 2, y_lo: 2; y = y_hi * 2 + y_lo), z: 16, core: 2. Of those that a mesh axis runs over, the one named last changes fastest.
Arguments:
- field: bfloat16 [20, 64, 64, 2048], P(None, 'gy', 'gz'), may hold values from -6 to 6
- cotangent: bfloat16 [20, 64, 64, 2048], P(None, 'gy', 'gz'), may hold values from -6 to 6
- spectral_weight: bfloat16 [576, 230400], P('gz', 'gy'), may hold values from -3 to 3
- point_weight: bfloat16 [20, 20], replicated, may hold values from -1.25 to 1.25
- channel_bias: float32 [20], replicated, may hold values from -3 to 3
Outputs:
- layer_output: bfloat16 [20, 64, 64, 2048], P(None, 'gy', 'gz')
- field_grad: bfloat16 [20, 64, 64, 2048], P(None, 'gy', 'gz')
- weight_grad: float32 [576, 230400], P('gz', 'gy')
All inputs are finite; a program needn't handle non-finite values.
Results may differ from a plain program's by a relative error of at most 0.02.
Values may be sent and summed in bfloat16 or wider, within the bound.
A program may use at most 128 MiB of HBM per device.

v0:
```python
import jax
import jax.numpy as jnp
from jax import lax
from jax.sharding import PartitionSpec as P

MODES = 12
NX = 64
NY = 64
NZ = 64
NT = 32
NKXT = 288
NKYZ = 576


full_turn = 6.283185307179586


def kept_slot(slots, length):
    return jnp.where(slots < MODES, slots, length - 2 * MODES + slots)


def split_matrix(matrix):
    high_part = matrix.astype(jnp.bfloat16)
    low_part = (matrix - high_part.astype(jnp.float32)).astype(jnp.bfloat16)
    return (high_part, low_part)


def plane_matrix():
    cell_index = jnp.arange(NX * NT, dtype=jnp.int32)
    x_position = cell_index // NT
    t_position = cell_index % NT
    mode_index = jnp.arange(NKXT, dtype=jnp.int32)
    x_frequency = kept_slot(mode_index // MODES, NX)
    t_frequency = mode_index % MODES
    phases = (
        x_frequency[None, :] * x_position[:, None] % NX * NT
        + t_frequency[None, :] * t_position[:, None] % NT * NX
    ) % (NX * NT)
    angles = phases.astype(jnp.float32) * (full_turn / (NX * NT))
    matrix = jnp.stack([jnp.cos(angles), -jnp.sin(angles)], axis=-1)
    return matrix.reshape(NX * NT, NKXT * 2)


def pencil_tables(pair_first, pair_count, z_first, z_count):
    pair_index = pair_first + jnp.arange(pair_count, dtype=jnp.int32)
    y_frequency = kept_slot(pair_index // (2 * MODES), NY)
    z_frequency = kept_slot(pair_index % (2 * MODES), NZ)
    y_position = jnp.arange(NY, dtype=jnp.int32)
    z_position = z_first + jnp.arange(z_count, dtype=jnp.int32)
    phases = (
        y_frequency[:, None, None] * y_position[None, :, None] % NY * NZ
        + z_frequency[:, None, None] * z_position[None, None, :] % NZ * NY
    ) % (NY * NZ)
    angles = phases.astype(jnp.float32) * (full_turn / (NY * NZ))
    return (split_matrix(jnp.cos(angles)), split_matrix(jnp.sin(angles)))


def split_product(halves, right):
    return jnp.dot(halves[0], right, preferred_element_type=jnp.float32) + jnp.dot(
        halves[1], right, preferred_element_type=jnp.float32
    )


def split_product_first(halves, right):
    dims = (((0,), (0,)), ((), ()))
    return lax.dot_general(
        halves[0], right, dims, preferred_element_type=jnp.float32
    ) + lax.dot_general(halves[1], right, dims, preferred_element_type=jnp.float32)


def pencil_columns(pencils, channels, own_modes):
    rows_a, rows_b = (pencils.shape[1], pencils.shape[2])
    grouped = pencils.reshape(channels, rows_a, rows_b, own_modes, 2)
    return jnp.transpose(grouped, (1, 2, 4, 0, 3)).reshape(
        rows_a * rows_b, 2 * channels * own_modes
    )


def forward_combine(cosine_part, sine_part, amount):
    cosine_part = cosine_part.reshape(amount, 2, -1)
    sine_part = sine_part.reshape(amount, 2, -1)
    real_part = cosine_part[:, 0] + sine_part[:, 1]
    imag_part = cosine_part[:, 1] - sine_part[:, 0]
    return jnp.stack([real_part, imag_part], axis=1).reshape(amount, -1)


def per_device(field, cotangent, spectral_weight, point_weight, channel_bias):
    channels, rows_y, rows_z, cell_count = field.shape
    own_pairs = spectral_weight.shape[0]
    own_modes = spectral_weight.shape[1] // (2 * channels * channels)
    row_width = own_modes * 2 * channels
    pair_modes = own_pairs * own_modes
    z_first = lax.axis_index("gz") * rows_z
    plane_high, plane_low = split_matrix(plane_matrix())
    near_cos, near_sin = pencil_tables(0, NKYZ, z_first, rows_z)
    near_cos = (near_cos[0].reshape(NKYZ, NY * rows_z), near_cos[1].reshape(NKYZ, NY * rows_z))
    near_sin = (near_sin[0].reshape(NKYZ, NY * rows_z), near_sin[1].reshape(NKYZ, NY * rows_z))
    far_cos, far_sin = pencil_tables(lax.axis_index("gz") * own_pairs, own_pairs, 0, NZ)

    def analyse(values):
        flattened = values.reshape(channels * rows_y * rows_z, cell_count)
        projected = jnp.dot(flattened, plane_high, preferred_element_type=jnp.float32) + jnp.dot(
            flattened, plane_low, preferred_element_type=jnp.float32
        )
        projected = projected.astype(jnp.bfloat16).reshape(channels, rows_y, rows_z, NKXT * 2)
        pencils = lax.all_to_all(projected, "gy", split_axis=3, concat_axis=1, tiled=True)
        portion = lax.all_gather(pencils, "gz", axis=2, tiled=True)
        depth = portion.shape[2]
        columns = pencil_columns(portion, channels, own_modes)
        cos_part = tuple((h.reshape(own_pairs, NY * depth) for h in far_cos))
        sin_part = tuple((h.reshape(own_pairs, NY * depth) for h in far_sin))
        summed = forward_combine(
            split_product(cos_part, columns), split_product(sin_part, columns), own_pairs
        )
        return jnp.transpose(
            summed.reshape(own_pairs, 2, channels, own_modes), (1, 2, 0, 3)
        ).reshape(2, channels, pair_modes)

    def synthesise(coeffs):
        portion = lax.all_gather(coeffs, "gz", axis=0, tiled=True)
        cos_part = tuple((h for h in near_cos))
        sin_part = tuple((h for h in near_sin))
        cosine_part = split_product_first(cos_part, portion).reshape(
            NY * rows_z, 2, channels * own_modes
        )
        sine_part = split_product_first(sin_part, portion).reshape(
            NY * rows_z, 2, channels * own_modes
        )
        real_part = cosine_part[:, 0] - sine_part[:, 1]
        imag_part = sine_part[:, 0] + cosine_part[:, 1]
        planes = jnp.stack([real_part, imag_part], axis=1)
        planes = jnp.transpose(planes.reshape(NY, rows_z, 2, channels, own_modes), (3, 0, 1, 4, 2))
        planes = planes.astype(jnp.bfloat16).reshape(channels, NY, rows_z, own_modes * 2)
        returned = lax.all_to_all(planes, "gy", split_axis=1, concat_axis=3, tiled=True)
        flattened = returned.reshape(channels * rows_y * rows_z, NKXT * 2)
        dims = (((1,), (1,)), ((), ()))
        volume = lax.dot_general(
            flattened, plane_high, dims, preferred_element_type=jnp.float32
        ) + lax.dot_general(flattened, plane_low, dims, preferred_element_type=jnp.float32)
        return volume.reshape(channels, rows_y, rows_z, cell_count)

    def to_rows(values):
        return jnp.transpose(
            values.reshape(2, channels, own_pairs, own_modes), (2, 0, 1, 3)
        ).reshape(own_pairs, row_width)

    mode_index = lax.axis_index("gy") * own_modes + jnp.arange(own_modes, dtype=jnp.int32)
    scale_row = jnp.where(mode_index % MODES == 0, 1.0, 2.0).astype(jnp.float32) / (
        NX * NY * NZ * NT
    )
    scaling = jnp.broadcast_to(scale_row[None, :], (own_pairs, own_modes)).reshape(pair_modes)
    coeffs = analyse(field)
    kernel = jnp.transpose(
        spectral_weight.reshape(own_pairs, own_modes, 2, channels, channels), (2, 3, 4, 0, 1)
    )
    kernel = kernel.reshape(2, channels, channels, pair_modes).astype(jnp.float32)
    real_in, imag_in = (coeffs[0][:, None, :], coeffs[1][:, None, :])
    real_w, imag_w = (kernel[0], kernel[1])
    real_part = jnp.sum(real_in * real_w - imag_in * imag_w, axis=0)
    imag_part = jnp.sum(real_in * imag_w + imag_in * real_w, axis=0)
    spectrum_out = (jnp.stack([real_part, imag_part], axis=0) * scaling).astype(jnp.bfloat16)
    spectral_out = synthesise(to_rows(spectrum_out))
    preact = (
        spectral_out
        + jnp.einsum("io,iyzr->oyzr", point_weight, field, preferred_element_type=jnp.float32)
        + channel_bias[:, None, None, None]
    )
    normal_cdf = 0.5 * (1.0 + lax.erf(preact * 0.7071067811865476))
    density = jnp.exp(-0.5 * preact * preact) * 0.3989422804014327
    layer_output = (preact * normal_cdf).astype(jnp.bfloat16)
    slope_grad = (cotangent.astype(jnp.float32) * (normal_cdf + preact * density)).astype(
        jnp.bfloat16
    )
    grads = analyse(slope_grad) * scaling
    real_g, imag_g = (grads[0][None, :, :], grads[1][None, :, :])
    grad_real = real_in * real_g + imag_in * imag_g
    grad_imag = real_in * imag_g - imag_in * real_g
    weight_grad = jnp.stack([grad_real, grad_imag], axis=0).reshape(
        2, channels, channels, own_pairs, own_modes
    )
    weight_grad = jnp.transpose(weight_grad, (3, 4, 0, 1, 2)).reshape(
        own_pairs, own_modes * 2 * channels * channels
    )
    back_real = jnp.sum(real_w * real_g + imag_w * imag_g, axis=1)
    back_imag = jnp.sum(real_w * imag_g - imag_w * real_g, axis=1)
    mode_back = jnp.stack([back_real, back_imag], axis=0).astype(jnp.bfloat16)
    spectral_back = synthesise(to_rows(mode_back))
    field_grad = (
        spectral_back
        + jnp.einsum("io,oyzr->iyzr", point_weight, slope_grad, preferred_element_type=jnp.float32)
    ).astype(jnp.bfloat16)
    return (layer_output, field_grad, weight_grad)


def solution(mesh):
    return jax.shard_map(
        per_device,
        mesh=mesh,
        in_specs=(P(None, "gy", "gz", None), P(None, "gy", "gz", None), P("gz", "gy"), P(), P()),
        out_specs=(P(None, "gy", "gz", None), P(None, "gy", "gz", None), P("gz", "gy")),
        check_vma=False,
    )
```

profile of v0, /device:TPU:1, one launch (start us, length us, event | category | flops | bytes accessed | tf_op | source)
XLA Modules:
  0.0 553.1 jit_solution(8284190507888450446)
XLA Ops:
  7.3 11.3 %fusion.27 = (f32[2048,288,1]{0,1,2:T(8,128)S(1)}, f32[2048,288,1]{0,1,2:T(8,128)S(1)}) fusion(s32[2048]{0:T(1024)S(1)} %get-tuple-element.61, s32[288]{0:T(512)S(1)} %get-tuple-element.64, s32[2048]{0:T(1024)S(1)} %get-tuple-element.62, s32[288]{0:T(512)S(1)} %get-tuple-element.63), kind=kLoop, calls=%fused_computation.76 | loop fusion | flops 24182784 | bytes 4737280 | tf_op jit(solution)/shard_map/cos | solution.py:40
  21.3 3.9 copy.269
  25.2 5.0 convert_element_type.363
  32.2 5.5 copy.270
  37.7 6.1 %convert_element_type.366 = bf16[2048,576]{0,1:T(8,128)(2,1)} reshape(bf16[2048,288,2]{0,2,1:T(2,128)(2,1)} %copy.270) | data formatting | bytes 4718592 | tf_op jit(solution)/shard_map/convert_element_type | solution.py:24
  49.1 34.0 %all_to_all.66 = bf16[32,2,1440]{2,1,0:T(2,128)(2,1)S(1)} all-to-all(bf16[32,2,1440]{2,1,0:T(2,128)(2,1)S(1)} %reshape.911), channel_id=1, replica_groups=mesh['gy'=32,'gz'=16] {'gy'}, dimensions={0} | all-to-all | bytes 368640 | tf_op jit(solution)/shard_map/all_to_all | solution.py:106
  84.4 3.5 copy.348
  87.9 3.3 copy.273
  92.7 2.6 copy.283
  95.3 4.7 reshape.894
  100.0 3.9 fusion.101
  103.9 5.1 copy.287
  109.0 3.5 copy.284
  112.8 5.4 subtract_convert_fusion.1
  123.7 46.6 %all-gather.5.cloned.1.call-done = bf16[20,64,64,18]{1,0,3,2:T(8,128)(2,1)} async-done(((bf16[20,64,4,18]{1,0,3,2:T(8,128)(2,1)}), bf16[20,64,64,18]{1,0,3,2:T(8,128)(2,1)}) %all-gather.5.cloned.1.call-update) | async-done | bytes 2949136 | tf_op jit(solution)/shard_map/all_gather | solution.py:107
  170.3 10.3 %copy.276 = bf16[64,64,2,20,9]{1,0,4,3,2:T(8,128)(2,1)} copy(bf16[64,64,2,20,9]{0,3,2,4,1:T(8,128)(2,1)} %bitcast.199) | data formatting | bytes 5898240 | tf_op jit(solution)/shard_map/transpose | solution.py:74
  180.6 7.6 %reshape.871 = bf16[4096,360]{0,1:T(8,128)(2,1)S(1)} reshape(bf16[64,64,2,20,9]{1,0,4,3,2:T(8,128)(2,1)} %copy.276) | data formatting | bytes 5898240 | tf_op jit(solution)/shard_map/reshape | solution.py:74
  196.0 5.7 %fusion.1 = (f32[20,324]{0,1:T(8,128)S(1)}, f32[20,324]{0,1:T(8,128)S(1)}) fusion(f32[1,20,20,36,9]{2,1,4,3,0:T(8,128)} %copy.287, f32[1,20,20,36,9]{2,1,4,3,0:T(8,128)} %copy.284, f32[20,324]{0,1:T(8,128)S(1)} %reshape.904, f32[20,324]{0,1:T(8,128)S(1)} %reshape.903), kind=kLoop, calls=%fused_computation.14 | loop fusion | flops 1023840 | bytes 1140480 | tf_op jit(solution)/shard_map/reduce_sum | solution.py:159
  202.7 22.3 %all-gather = bf16[16,36,360]{2,1,0:T(8,128)(2,1)S(1)} all-gather(bf16[1,36,360]{2,1,0:T(8,128)(2,1)S(1)} %copy.293), channel_id=1, replica_groups=mesh['gy'=32,'gz'=16] {'gz'}, dimensions={0}, use_global_device_ids=true | all-gather | bytes 440640 | tf_op jit(solution)/shard_map/all_gather | solution.py:120
  230.4 2.7 convolution_add_fusion.7
  233.1 2.6 convolution_add_fusion.8
  237.1 2.9 copy.297
  241.1 2.9 copy.296
  246.8 31.1 %all_to_all.67 = bf16[32,2,1440]{2,1,0:T(2,128)(2,1)S(1)} all-to-all(bf16[32,2,1440]{2,1,0:T(2,128)(2,1)S(1)} %reshape.913), channel_id=1, replica_groups=mesh['gy'=32,'gz'=16] {'gy'}, dimensions={0} | all-to-all | bytes 368640 | tf_op jit(solution)/shard_map/all_to_all | solution.py:134
  279.4 4.0 copy.301
  283.4 3.2 reshape.878
  290.0 2.7 reshape.879
  292.7 5.0 fusion.21
  306.8 20.5 %all_to_all.68 = bf16[32,2,1440]{2,1,0:T(2,128)(2,1)S(1)} all-to-all(bf16[32,2,1440]{2,1,0:T(2,128)(2,1)S(1)} %reshape.915), channel_id=1, replica_groups=mesh['gy'=32,'gz'=16] {'gy'}, dimensions={0} | all-to-all | bytes 368640 | tf_op jit(solution)/shard_map/all_to_all | solution.py:106
  328.6 3.5 copy.357
  332.1 3.3 copy.309
  336.9 75.5 %all-gather.7.cloned.1.call-done = bf16[20,64,64,18]{1,0,3,2:T(8,128)(2,1)} async-done(((bf16[20,64,4,18]{1,0,3,2:T(8,128)(2,1)}), bf16[20,64,64,18]{1,0,3,2:T(8,128)(2,1)}) %all-gather.7.cloned.1.call-update) | async-done | bytes 2949136 | tf_op jit(solution)/shard_map/all_gather | solution.py:107
  412.5 10.3 %copy.312 = bf16[64,64,2,20,9]{1,0,4,3,2:T(8,128)(2,1)} copy(bf16[64,64,2,20,9]{0,3,2,4,1:T(8,128)(2,1)} %bitcast.200) | data formatting | bytes 5898240 | tf_op jit(solution)/shard_map/transpose | solution.py:74
  422.7 7.7 %reshape.883 = bf16[4096,360]{0,1:T(8,128)(2,1)S(1)} reshape(bf16[64,64,2,20,9]{1,0,4,3,2:T(8,128)(2,1)} %copy.312) | data formatting | bytes 5898240 | tf_op jit(solution)/shard_map/reshape | solution.py:74
  437.4 8.1 %bitcast_multiply_fusion.5 = (f32[20,20,324]{1,0,2:T(8,128)}, f32[20,20,324]{1,0,2:T(8,128)S(1)}, f32[20,20,324]{1,0,2:T(8,128)}, f32[20,20,324]{1,0,2:T(8,128)}) fusion(f32[1,20,20,36,9]{2,1,4,3,0:T(8,128)} %copy.284, f32[20,324]{0,1:T(8,128)S(1)} %bitcast.217, f32[20,324]{0,1:T(8,128)S(1)} %bitcast.218, f32[1,20,20,36,9]{2,1,4,3,0:T(8,128)} %copy.287), kind=kLoop, calls=%fused_computation.18 | loop fusion | flops 518400 | bytes 3162240 | tf_op jit(solution)/shard_map/mul | solution.py:184
  445.5 3.3 subtract_reduce_fusion
  449.5 4.5 add_reduce_fusion
  455.1 22.0 %all-gather.1 = bf16[16,36,360]{2,1,0:T(8,128)(2,1)S(1)} all-gather(bf16[1,36,360]{2,1,0:T(8,128)(2,1)S(1)} %copy.327), channel_id=1, replica_groups=mesh['gy'=32,'gz'=16] {'gz'}, dimensions={0}, use_global_device_ids=true | all-gather | bytes 440640 | tf_op jit(solution)/shard_map/all_gather | solution.py:120
  482.6 2.7 convolution_add_fusion.5
  485.3 2.6 convolution_add_fusion.6
  489.4 2.9 copy.331
  493.4 2.9 copy.330
  499.7 13.5 %all-to-all-start.3 = ((bf16[32,2,1440]{2,1,0:T(2,128)(2,1)}), bf16[32,2,1440]{2,1,0:T(2,128)(2,1)S(1)}, u32[]{:S(2)}, u32[]{:S(2)}) async-start(bf16[32,2,1440]{2,1,0:T(2,128)(2,1)} %reshape.917), calls=%async_computation.3 | async-start | bytes 393216 | tf_op jit(solution)/shard_map/all_to_all | solution.py:134
  518.1 4.7 reshape.893
  522.8 3.5 copy.345
  526.3 5.0 all-to-all-done.3
  532.9 4.0 copy.335
  536.8 3.2 reshape.891
  (200 shorter events, 86.5 us)
Async XLA Ops:
  7.2 285.6 %copy-start = (bf16[20,20]{1,0:T(8,128)(2,1)S(1)}, bf16[20,20]{1,0:T(8,128)(2,1)}, u32[]{:S(2)}) copy-start(bf16[20,20]{1,0:T(8,128)(2,1)} %param.8) | copy-start | bytes 2404
  7.2 163.1 %all-gather.5.cloned.1.call-start = ((), (), s32[]{:S(2)}) async-start(), calls=%async_computation.4 | async-start | bytes 7520256 | tf_op jit(solution)/shard_map/all_gather | solution.py:107
  30.3 13.6 %copy-start.1 = (bf16[2048,576]{0,1:T(8,128)(2,1)}, bf16[2048,576]{0,1:T(8,128)(2,1)S(1)}, u32[]{:S(2)}) copy-start(bf16[2048,576]{0,1:T(8,128)(2,1)S(1)} %convert_element_type.363) | copy-start | bytes 7077892
  43.8 1.7 copy-start.4
  87.9 4.7 copy-start.24
  92.6 319.9 %all-gather.7.cloned.1.call-start = ((), (), s32[]{:S(2)}) async-start(), calls=%async_computation.5 | async-start | bytes 7520256 | tf_op jit(solution)/shard_map/all_gather | solution.py:107
  122.3 71.1 %copy-start.10 = (bf16[36,4096]{1,0:T(8,128)(2,1)}, bf16[36,4096]{1,0:T(8,128)(2,1)S(1)}, u32[]{:S(2)}) copy-start(bf16[36,4096]{1,0:T(8,128)(2,1)S(1)} %convert_element_type.376) | copy-start | bytes 884740
  188.2 2.0 copy-start.12
  195.5 6.3 %copy-start.16 = (f32[1,20,36,9]{2,0,3,1:T(1,128)}, f32[1,20,36,9]{2,0,3,1:T(1,128)S(1)}, u32[]{:S(2)}) copy-start(f32[1,20,36,9]{2,0,3,1:T(1,128)S(1)} %get-tuple-element.43) | copy-start | bytes 77764
  195.5 6.3 %copy-start.18 = (f32[1,20,36,9]{2,0,3,1:T(1,128)}, f32[1,20,36,9]{2,0,3,1:T(1,128)S(1)}, u32[]{:S(2)}) copy-start(f32[1,20,36,9]{2,0,3,1:T(1,128)S(1)} %get-tuple-element.44) | copy-start | bytes 77764
  201.8 23.3 %copy-start.22 = (s32[576,256]{0,1:T(8,128)S(1)}, s32[576,256]{0,1:T(8,128)}, u32[]{:S(2)}) copy-start(s32[576,256]{0,1:T(8,128)} %add.508) | copy-start | bytes 1769476
  279.4 7.2 %copy-start.2 = (bf16[2048,576]{0,1:T(8,128)(2,1)S(1)}, bf16[2048,576]{0,1:T(8,128)(2,1)}, u32[]{:S(2)}) copy-start(bf16[2048,576]{0,1:T(8,128)(2,1)} %copy-done.1) | copy-start | bytes 7077892
  286.6 1.7 copy-start.5
  290.0 2.7 copy-start.21
  290.0 2.7 copy-start.25
  297.7 0.9 copy-start.8
  301.5 1.7 copy-start.6
  422.7 7.7 %copy-start.14 = (bf16[36,4096]{1,0:T(8,128)(2,1)S(1)}, bf16[36,4096]{1,0:T(8,128)(2,1)}, u32[]{:S(2)}) copy-start(bf16[36,4096]{1,0:T(8,128)(2,1)} %convert_element_type.360) | copy-start | bytes 884740
  430.4 1.0 copy-start.15
  431.4 1.0 copy-start.13
  432.4 1.3 copy-start.11
  454.0 23.3 %copy-start.23 = (s32[576,256]{0,1:T(8,128)S(1)}, s32[576,256]{0,1:T(8,128)}, u32[]{:S(2)}) copy-start(s32[576,256]{0,1:T(8,128)} %add.508) | copy-start | bytes 1769476
  496.3 17.0 %copy-start.19 = (f32[1,20,36,9]{2,0,3,1:T(1,128)S(1)}, f32[1,20,36,9]{2,0,3,1:T(1,128)}, u32[]{:S(2)}) copy-start(f32[1,20,36,9]{2,0,3,1:T(1,128)} %copy-done.18) | copy-start | bytes 77764
  496.3 17.0 %copy-start.17 = (f32[1,20,36,9]{2,0,3,1:T(1,128)S(1)}, f32[1,20,36,9]{2,0,3,1:T(1,128)}, u32[]{:S(2)}) copy-start(f32[1,20,36,9]{2,0,3,1:T(1,128)} %copy-done.16) | copy-start | bytes 77764
  496.6 16.7 %copy-start.20 = (bf16[20,2,4,2048]{3,0,2,1:T(8,128)(2,1)S(1)}, bf16[20,2,4,2048]{3,0,2,1:T(8,128)(2,1)}, u32[]{:S(2)}) copy-start(bf16[20,2,4,2048]{3,0,2,1:T(8,128)(2,1)} %get-tuple-element.32) | copy-start | bytes 1966084
  499.7 31.5 %all-to-all-start.3 = ((bf16[32,2,1440]{2,1,0:T(2,128)(2,1)}), bf16[32,2,1440]{2,1,0:T(2,128)(2,1)S(1)}, u32[]{:S(2)}, u32[]{:S(2)}) async-start(bf16[32,2,1440]{2,1,0:T(2,128)(2,1)} %reshape.917), calls=%async_computation.3 | async-start | bytes 393216 | tf_op jit(solution)/shard_map/all_to_all | solution.py:134
  532.9 7.2 %copy-start.3 = (bf16[2048,576]{0,1:T(8,128)(2,1)S(1)}, bf16[2048,576]{0,1:T(8,128)(2,1)}, u32[]{:S(2)}) copy-start(bf16[2048,576]{0,1:T(8,128)(2,1)} %copy-done.1) | copy-start | bytes 7077892
  540.0 1.7 copy-start.7
  542.4 1.1 copy-start.9
Sparse Core Ops, SparseCore 0:
  92.7 77.5 all-gather.4
  336.9 75.4 all-gather.6
where the time goes:
time: 564 us; the launch traced here: 553 us
  local copies, waits for them, and re-layouts  175 us (31%)
  blocking collectives  130 us (23%)
  waiting for transfers between devices  127 us (23%)
  other arithmetic  47.1 us (8%)
  matrix products  44.6 us (8%)
  between operations  15.7 us (3%)
  starting transfers between devices  13.5 us (2%)
    all_gather x2, waiting for transfers between devices, analyse(): portion = lax.all_gather(pencils, 'gz', axis=2, tiled=True)  122 us
    all_to_all x2, blocking collectives, analyse(): lax.all_to_all(projected, 'gy', split_axis=3, concat_axis=1, tiled=True)  54.5 us
    all_gather x2, blocking collectives, synthesise(): portion = lax.all_gather(coeffs, 'gz', axis=0, tiled=True)  44.3 us
    all_to_all x1, blocking collectives, synthesise(): lax.all_to_all(planes, 'gy', split_axis=1, concat_axis=3, tiled=True)  31.1 us
    unnamed x77, local copies, waits for them, and re-layouts  24.3 us
    transpose x2, local copies, waits for them, and re-layouts, pencil_columns(): jnp.transpose(grouped, (1, 2, 4, 0, 3))  20.5 us
    all_to_all x6, local copies, waits for them, and re-layouts, analyse(): lax.all_to_all(projected, 'gy', split_axis=3, concat_axis=1, tiled=True)  16.3 us
    another operation x8, local copies, waits for them, and re-layouts, synthesise(): planes = jnp.stack([real_part, imag_part], axis=1)  15.9 us
  transfers between devices with their start and end apart: 3, of which 3 were waited for; matrix products, arithmetic and copies ran while one was open for 8% of the time, Pallas kernels for 0%

commit v1 on v0

v1 whole, which is shorter than its diff:
```python
import functools

import jax
import jax.numpy as jnp
import ml_dtypes
import numpy as np
from jax import lax
from jax.experimental import pallas as pl
from jax.experimental.pallas import tpu as pltpu
from jax.sharding import PartitionSpec as P

MODES = 12
NX = 64
NY = 64
NZ = 64
NT = 32
CH = 20
GY = 32
GZ = 16
PAIRS = 36
PROWS = 40
SLAB = 24
MESH = pl.DeviceIdType.MESH
BF = jnp.bfloat16
F32 = jnp.float32


def kept(slots, length):
    return np.where(slots < MODES, slots, length - 2 * MODES + slots)


def plane_constant():
    cell = np.arange(NX * NT)
    x, t = cell // NT, cell % NT
    out = np.zeros((GY, 3, 8, NX * NT))
    for d in range(GY):
        for k in range(3):
            for q3 in range(3):
                q = 9 * d + 3 * k + q3
                kx, kt = kept(np.array(q // MODES), NX), q % MODES
                angle = 2 * np.pi * ((kx * x % NX) / NX + (kt * t % NT) / NT)
                out[d, k, 2 * q3] = np.cos(angle)
                out[d, k, 2 * q3 + 1] = -np.sin(angle)
    return out.reshape(GY * SLAB, NX * NT)


def slot_frequency(length):
    g = np.arange(GZ)[:, None]
    return kept(3 * g // 2 + np.arange(2)[None, :], length)


def on_slabs(cosine, sine):
    rows, cols = cosine.shape
    two = np.stack([np.stack([cosine, sine], -1), np.stack([-sine, cosine], -1)], 2)
    full = np.einsum("rcab,uv->ruacvb", two.transpose(0, 1, 2, 3), np.eye(12))
    return full.reshape(rows * SLAB, cols * SLAB)


def y_constants():
    ky = slot_frequency(NY)
    y = 2 * np.arange(GY)[None, :] + np.arange(2)[:, None]
    angle = 2 * np.pi * (ky[None, :, :, None] * y[:, None, None, :] % NY) / NY
    near = angle.transpose(0, 2, 1, 3)
    forward = on_slabs(np.cos(near).reshape(-1, GY), np.sin(near).reshape(-1, GY))
    far = angle.transpose(0, 2, 3, 1)
    back = on_slabs(np.cos(far).reshape(-1, GZ), -np.sin(far).reshape(-1, GZ))
    return forward, back


def pair_slots(parity):
    p = np.arange(PAIRS) + 12 * parity
    return p // 24, p % 24


def z_constants():
    forward = np.zeros((2, 4, 2, 3, 168, GZ, 12, 2))
    back = np.zeros((2, 4, GZ, 12, 2, 2, 3, 168))
    for parity in range(2):
        kz = kept(pair_slots(parity)[1], NZ)
        for zl in range(4):
            angle = 2 * np.pi * (kz[:, None] * (4 * np.arange(GZ) + zl)[None, :] % NZ) / NZ
            c, s = np.cos(angle), np.sin(angle)
            for k in range(3):
                for q3 in range(4):
                    rows = slice(PROWS * q3, PROWS * q3 + PAIRS) if q3 < 3 else slice(128, 128 + PAIRS)
                    u = 4 * k + q3
                    forward[parity, zl, 0, k, rows, :, u, 0] = c
                    forward[parity, zl, 0, k, rows, :, u, 1] = s
                    forward[parity, zl, 1, k, rows, :, u, 0] = -s
                    forward[parity, zl, 1, k, rows, :, u, 1] = c
                    back[parity, zl, :, u, 0, 0, k, rows] = c.T
                    back[parity, zl, :, u, 0, 1, k, rows] = -s.T
                    back[parity, zl, :, u, 1, 0, k, rows] = s.T
                    back[parity, zl, :, u, 1, 1, k, rows] = c.T
    back = np.pad(back.reshape(2, 4 * GZ * SLAB, 1008), ((0, 0), (0, 0), (0, 16)))
    return forward.reshape(2, 4 * 1008, GZ * SLAB), back


def mask_constant():
    lane = np.arange(128)
    out = np.zeros((2, 2, 128, 128))
    for parity in range(2):
        slot = pair_slots(parity)[0]
        for q3 in range(3):
            rows = slice(PROWS * q3, PROWS * q3 + PAIRS)
            match = (lane // 4 % 2)[None, :] == slot[:, None]
            out[parity, 0, rows] = match
            out[parity, 1, rows] = match & (lane // 32 == q3)[None, :]
    return out


def channel_constants():
    lane = np.arange(128)
    channel = np.concatenate([lane // 8, np.where(lane < 96, 16 + lane % 32 // 8, -1)])
    pair = np.arange(512)
    first = np.where(pair < CH * CH, pair // CH, -2)
    second = np.where(pair < CH * CH, pair % CH, -2)
    return channel[:, None] == first[None, :], channel[:, None] == second[None, :]


@functools.cache
def constants():
    half = lambda a: np.asarray(a, np.float32).astype(ml_dtypes.bfloat16)
    y_forward, y_back = y_constants()
    z_forward, z_back = z_constants()
    first, second = channel_constants()
    spread = np.stack([first, second])
    return (
        half(plane_constant()),
        half(y_forward),
        half(z_forward),
        half(z_back),
        half(y_back),
        half(spread),
        half(spread.transpose(0, 2, 1)),
        np.asarray(mask_constant(), np.float32),
    )


def dot(a, b):
    return jnp.dot(a, b, preferred_element_type=F32)


def dot_t(a, b):
    return lax.dot_general(a, b, (((1,), (1,)), ((), ())), preferred_element_type=F32)


def lanes(shape):
    return lax.broadcasted_iota(jnp.int32, shape, len(shape) - 1)


def kernel(
    field_hbm, cot_hbm, weight_hbm, point_ref, bias_ref,
    plane_hbm, yf_hbm, zf_hbm, zb_hbm, yb_hbm, spread_hbm, gather_hbm, mask_hbm,
    out_hbm, fgrad_hbm, wgrad_hbm,
    field, cot, weight, plane, yf, zf, zb, yb, spread, gather, mask,
    slope, layer, fgrad, wf, w0, w1, u0, u1, wg, wgrad, turned, scale, point_fwd, point_bwd, bias_col,
    sy, ry, sz, rz, szb, rzb, syb, ryb, load_sem, store_sem, send_sem, recv_sem,
):
    j = lax.axis_index("gy")
    g = lax.axis_index("gz")
    parity = lax.rem(g, 2)

    def load(i, src, dst):
        copy = pltpu.make_async_copy(src, dst, load_sem.at[i])
        copy.start()
        return copy

    got_field = load(0, field_hbm, field.at[pl.ds(0, 160)])
    got_plane = load(1, plane_hbm, plane)
    got_yf = load(2, yf_hbm, yf)
    got_weight = load(3, weight_hbm, weight)
    got_zf = load(4, zf_hbm.at[parity], zf)
    got_spread = load(5, spread_hbm, spread)
    got_gather = load(6, gather_hbm, gather)
    got_mask = load(7, mask_hbm.at[parity], mask)
    got_zb = load(8, zb_hbm.at[parity], zb)
    got_yb = load(9, yb_hbm, yb)
    got_cot = load(10, cot_hbm, cot)

    barrier = pltpu.get_barrier_semaphore()

    def greet(axis, me, count):
        def one(k, carry):
            pl.semaphore_signal(barrier, inc=1, device_id={axis: lax.rem(me + k, count)}, device_id_type=MESH)
            return carry

        lax.fori_loop(1, count, one, 0)

    greet("gy", j, GY)
    greet("gz", g, GZ)

    def send(src, dst, axis, me, count, which):
        def one(k, carry):
            other = lax.rem(me + k, count)
            pltpu.make_async_remote_copy(
                src_ref=src.at[other],
                dst_ref=dst.at[me],
                send_sem=send_sem.at[which],
                recv_sem=recv_sem.at[which],
                device_id={axis: other},
                device_id_type=MESH,
            ).start()
            return carry

        lax.fori_loop(1, count, one, 0)
        dst[pl.ds(me, 1)] = src[pl.ds(me, 1)]

    def arrive(src, dst, count, which):
        part = pl.ds(0, count - 1)
        pltpu.make_async_copy(dst.at[part], dst.at[part], recv_sem.at[which]).wait()
        pltpu.make_async_copy(src.at[part], src.at[part], send_sem.at[which]).wait()

    zlane = lanes((1, 128)) % 4
    low_slot = lanes((1, 128)) // 4 % 2 == 0
    row3 = lax.broadcasted_iota(jnp.int32, (1, 8, 128), 1)
    lane3 = lanes((1, 8, 128))

    def planes_out(source, buffer):
        full = dot_t(plane[...], source[...])
        main = full[:, :128].reshape(96, 8, 128)
        left = full[:, 128:].reshape(96, 8, 128)
        extra = jnp.zeros_like(main)
        for q3 in range(3):
            moved = pltpu.roll(left, 6 - 2 * q3, 1)
            if q3:
                moved = pltpu.roll(moved, 32 * q3, 2)
            extra = jnp.where(lane3 // 32 == q3, moved, extra)
        buffer[...] = jnp.where(row3 >= 6, extra, main).reshape(GY, SLAB, 128).astype(BF)

    def planes_in(buffer):
        block = buffer[...].astype(F32).reshape(96, 8, 128)
        left = jnp.zeros_like(block)
        for q3 in range(3):
            moved = pltpu.roll(block, 2 + 2 * q3, 1)
            if q3:
                moved = pltpu.roll(moved, 128 - 32 * q3, 2)
            left = jnp.where(row3 // 2 == q3, moved, left)
        turned[0:128] = block.reshape(768, 128).T.astype(BF)
        turned[128:256] = left.reshape(768, 128).T.astype(BF)

    def swap_slots(same_low, same_high, cross_low, cross_high):
        crossed = jnp.where(low_slot, pltpu.roll(cross_low, 124, 1), pltpu.roll(cross_high, 4, 1))
        return jnp.where(low_slot, same_low, same_high) + crossed

    def y_forward(buffer, target):
        block = buffer[...].reshape(768, 128)
        part = [dot(yf[384 * n : 384 * n + 384], block) for n in range(4)]
        target[...] = swap_slots(part[0], part[3], part[2], part[1]).reshape(GZ, SLAB, 128).astype(BF)

    def y_back(buffer, target):
        block = buffer[...].reshape(384, 128)
        part = [dot(yb[768 * n : 768 * n + 768], block) for n in range(4)]
        target[...] = swap_slots(part[0], part[3], part[1], part[2]).reshape(GY, SLAB, 128).astype(BF)

    def by_z(parts):
        low = jnp.where(zlane == 0, parts[0], parts[1])
        high = jnp.where(zlane == 2, parts[2], parts[3])
        return jnp.where(zlane < 2, low, high)

    def z_forward(buffer, factor):
        block = buffer[...].reshape(384, 128)
        values = by_z([dot(zf[1008 * n : 1008 * n + 1008], block) for n in range(4)]).reshape(6, 168, 128)
        left = values[:, 128:]
        left = jnp.concatenate([left, left, left, jnp.zeros((6, 8, 128), F32)], axis=1)
        main = (values[:, :128] * mask[0:1]).reshape(768, 128)
        left = (left * mask[1:2]).reshape(768, 128)
        if factor is not None:
            main, left = main * factor, left * factor
        return jnp.concatenate([main.astype(BF), left.astype(BF)], axis=1)

    def z_back(mixed, n, factor, target):
        values = dot(mixed, gather[n])
        if factor is not None:
            values = values * jnp.concatenate([factor, factor], axis=1)
        main = values[:, :128].reshape(6, 128, 128) * mask[0:1]
        left = values[:, 128:].reshape(6, 128, 128) * mask[1:2]
        left = left[:, 0:40] + left[:, 40:80] + left[:, 80:120]
        rows = jnp.concatenate([main, left], axis=1).reshape(1008, 128)
        rows = jnp.concatenate([rows, jnp.zeros((16, 128), F32)], axis=0).astype(BF)
        parts = [dot(zb[384 * n : 384 * n + 384], rows) for n in range(4)]
        target[...] = by_z(parts).reshape(GZ, SLAB, 128).astype(BF)

    field[160:256] = jnp.zeros((96, 2048), BF)
    slope[160:256] = jnp.zeros((96, 2048), BF)

    got_field.wait()
    got_plane.wait()
    planes_out(field, sy.at[0])
    pl.semaphore_wait(barrier, GY + GZ - 2)
    send(sy.at[0], ry.at[0], "gy", j, GY, 0)

    got_weight.wait()
    wf[...] = jnp.zeros((PROWS, 7296), F32)
    wf[0:PAIRS, 0:7200] = weight[...].astype(F32)
    w0[...] = jnp.zeros((384, 512), F32)
    w1[...] = jnp.zeros((384, 512), F32)
    for q in range(9):
        for part, held in enumerate((w0, w1)):
            start = 800 * q + 400 * part
            first, shift = start // 128 * 128, start % 128
            piece = wf[:, first : first + 512]
            if shift:
                piece = pltpu.roll(piece, 512 - shift, 1)
            top = 128 * (q // 3) + PROWS * (q % 3)
            held[top : top + PROWS] = piece
    row = lax.broadcasted_iota(jnp.int32, (384, 128), 0)
    inner = row % 128
    mode = 9 * j + 3 * (row // 128) + (inner >= 40).astype(jnp.int32) + (inner >= 80).astype(jnp.int32)
    factor = jnp.where(mode % MODES == 0, 1.0, 2.0) * (1.0 / (NX * NY * NZ * NT))
    scale[0:384] = factor
    scale[384:768] = factor
    copies = (lax.broadcasted_iota(jnp.int32, (160, CH), 0) // 8 == lanes((160, CH))).astype(F32)
    copies_half = copies.astype(BF)
    same_row = lax.broadcasted_iota(jnp.int32, (160, 160), 0) % 8 == lanes((160, 160)) % 8
    by_out = dot_t(copies_half, point_ref[...]).astype(BF)
    by_in = dot(copies_half, point_ref[...]).astype(BF)
    point_fwd[...] = jnp.where(same_row, dot_t(by_out, copies_half), 0.0).astype(BF)
    point_bwd[...] = jnp.where(same_row, dot_t(by_in, copies_half), 0.0).astype(BF)
    bias_col[...] = jnp.broadcast_to(jnp.sum(copies * bias_ref[...], axis=1, keepdims=True), (160, 128))

    got_yf.wait()
    arrive(sy.at[0], ry.at[0], GY, 0)
    y_forward(ry.at[0], sz.at[0])
    send(sz.at[0], rz.at[0], "gz", g, GZ, 1)
    got_zf.wait()
    got_spread.wait()
    got_gather.wait()
    got_mask.wait()
    arrive(sz.at[0], rz.at[0], GZ, 1)
    spread_u = dot(z_forward(rz.at[0], None), spread[0])
    real_u, imag_u = spread_u[:384], spread_u[384:]
    u0[...] = real_u
    u1[...] = imag_u
    mixed_real = (real_u * w0[...] - imag_u * w1[...]).astype(BF)
    mixed_imag = (real_u * w1[...] + imag_u * w0[...]).astype(BF)
    mixed = jnp.concatenate([mixed_real, mixed_imag], axis=0)
    got_zb.wait()
    z_back(mixed, 1, scale[...], szb.at[0])
    send(szb.at[0], rzb.at[0], "gz", g, GZ, 2)
    got_yb.wait()
    arrive(szb.at[0], rzb.at[0], GZ, 2)
    y_back(rzb.at[0], syb.at[0])
    send(syb.at[0], ryb.at[0], "gy", j, GY, 3)
    got_cot.wait()
    arrive(syb.at[0], ryb.at[0], GY, 3)
    planes_in(ryb.at[0])

    def activate(n, carry):
        cells = pl.ds(pl.multiple_of(n * 256, 256), 256)
        preact = dot(turned[0:160], plane[:, cells]) + dot(point_fwd[...], field[0:160, cells]) + bias_col[:, 0:1]
        normal = 0.5 * (1.0 + lax.erf(preact * 0.7071067811865476))
        density = jnp.exp(-0.5 * preact * preact) * 0.3989422804014327
        layer[:, cells] = (preact * normal).astype(BF)
        slope[0:160, cells] = (cot[:, cells].astype(F32) * (normal + preact * density)).astype(BF)
        return carry

    lax.fori_loop(0, 8, activate, 0)
    planes_out(slope, sy.at[1])
    send(sy.at[1], ry.at[1], "gy", j, GY, 4)
    put_layer = pltpu.make_async_copy(layer, out_hbm, store_sem.at[0])
    put_layer.start()
    arrive(sy.at[1], ry.at[1], GY, 4)
    y_forward(ry.at[1], sz.at[1])
    send(sz.at[1], rz.at[1], "gz", g, GZ, 5)
    arrive(sz.at[1], rz.at[1], GZ, 5)
    spread_g = dot(z_forward(rz.at[1], scale[...]), spread[1])
    real_g, imag_g = spread_g[:384], spread_g[384:]
    mixed_real = (real_g * w0[...] + imag_g * w1[...]).astype(BF)
    mixed_imag = (imag_g * w0[...] - real_g * w1[...]).astype(BF)
    mixed = jnp.concatenate([mixed_real, mixed_imag], axis=0)
    z_back(mixed, 0, None, szb.at[1])
    send(szb.at[1], rzb.at[1], "gz", g, GZ, 6)
    w0[...] = u0[...] * real_g + u1[...] * imag_g
    w1[...] = u0[...] * imag_g - u1[...] * real_g
    arrive(szb.at[1], rzb.at[1], GZ, 6)
    y_back(rzb.at[1], syb.at[1])
    send(syb.at[1], ryb.at[1], "gy", j, GY, 7)
    wg[...] = jnp.zeros((PROWS, 7296), F32)
    for q in range(9):
        for part, held in enumerate((w0, w1)):
            start = 800 * q + 400 * part
            first, shift = start // 128 * 128, start % 128
            top = 128 * (q // 3) + PROWS * (q % 3)
            piece = held[top : top + PROWS]
            if shift:
                piece = pltpu.roll(piece, shift, 1)
            wg[:, first : first + 512] = wg[:, first : first + 512] + piece
    wgrad[...] = wg[0:PAIRS, 0:7200]
    put_wgrad = pltpu.make_async_copy(wgrad, wgrad_hbm, store_sem.at[1])
    put_wgrad.start()
    arrive(syb.at[1], ryb.at[1], GY, 7)
    planes_in(ryb.at[1])

    def finish(n, carry):
        cells = pl.ds(pl.multiple_of(n * 256, 256), 256)
        total = dot(turned[0:160], plane[:, cells]) + dot(point_bwd[...], slope[0:160, cells])
        fgrad[:, cells] = total.astype(BF)
        return carry

    lax.fori_loop(0, 8, finish, 0)
    put_fgrad = pltpu.make_async_copy(fgrad, fgrad_hbm, store_sem.at[2])
    put_fgrad.start()
    put_layer.wait()
    put_wgrad.wait()
    put_fgrad.wait()


def per_device(field, cotangent, spectral_weight, point_weight, channel_bias):
    cells = NX * NT
    flat = field.reshape(160, cells)
    flat_cot = cotangent.reshape(160, cells)
    whole = pl.BlockSpec(memory_space=pltpu.VMEM)
    anywhere = pl.BlockSpec(memory_space=pl.ANY)
    consts = constants()
    vm = pltpu.VMEM
    scratch = [
        vm((256, cells), BF),
        vm((160, cells), BF),
        vm((PAIRS, 7200), BF),
        vm((768, cells), BF),
        vm((1536, 768), BF),
        vm((4032, 384), BF),
        vm((1536, 1024), BF),
        vm((3072, 384), BF),
        vm((2, 256, 512), BF),
        vm((2, 512, 256), BF),
        vm((2, 128, 128), F32),
        vm((256, cells), BF),
        vm((160, cells), BF),
        vm((160, cells), BF),
        vm((PROWS, 7296), F32),
        vm((384, 512), F32),
        vm((384, 512), F32),
        vm((384, 512), F32),
        vm((384, 512), F32),
        vm((PROWS, 7296), F32),
        vm((PAIRS, 7200), F32),
        vm((256, 768), BF),
        vm((768, 128), F32),
        vm((160, 160), BF),
        vm((160, 160), BF),
        vm((160, 128), F32),
        vm((2, GY, SLAB, 128), BF),
        vm((2, GY, SLAB, 128), BF),
        vm((2, GZ, SLAB, 128), BF),
        vm((2, GZ, SLAB, 128), BF),
        vm((2, GZ, SLAB, 128), BF),
        vm((2, GZ, SLAB, 128), BF),
        vm((2, GY, SLAB, 128), BF),
        vm((2, GY, SLAB, 128), BF),
        pltpu.SemaphoreType.DMA((11,)),
        pltpu.SemaphoreType.DMA((3,)),
        pltpu.SemaphoreType.DMA((8,)),
        pltpu.SemaphoreType.DMA((8,)),
    ]
    layer, fgrad, wgrad = pl.pallas_call(
        kernel,
        out_shape=(
            jax.ShapeDtypeStruct((160, cells), BF),
            jax.ShapeDtypeStruct((160, cells), BF),
            jax.ShapeDtypeStruct((PAIRS, 7200), F32),
        ),
        in_specs=[anywhere, anywhere, anywhere, whole, whole] + [anywhere] * len(consts),
        out_specs=(anywhere, anywhere, anywhere),
        scratch_shapes=scratch,
        compiler_params=pltpu.CompilerParams(
            collective_id=0, has_side_effects=True, vmem_limit_bytes=60 * 1024 * 1024
        ),
    )(flat, flat_cot, spectral_weight, point_weight, channel_bias.reshape(1, CH), *consts)
    return layer.reshape(field.shape), fgrad.reshape(field.shape), wgrad


def solution(mesh):
    return jax.shard_map(
        per_device,
        mesh=mesh,
        in_specs=(P(None, "gy", "gz", None), P(None, "gy", "gz", None), P("gz", "gy"), P(), P()),
        out_specs=(P(None, "gy", "gz", None), P(None, "gy", "gz", None), P("gz", "gy")),
        check_vma=False,
    )
```

time: 564 us -> 122 us (0.22); the launches traced: 553 us -> 122 us
  local copies, waits for them, and re-layouts: 175 us -> 10 us
  blocking collectives: 130 us -> 0 us
  waiting for transfers between devices: 127 us -> 0 us
  Pallas kernels: 0 us -> 111 us
  other arithmetic: 47.1 us -> 0 us
  matrix products: 44.6 us -> 0 us
  between operations: 15.7 us -> 0.65 us
  starting transfers between devices: 13.5 us -> 0 us
    all_gather x2 -> x0, waiting for transfers between devices: 122 us -> none  [analyse(): portion = lax.all_gather(pencils, 'gz', axis=2, tiled=True)]
    pallas_call x0 -> x1, Pallas kernels: none -> 111 us  [per_device(): pl.pallas_call(kernel, out_shape=(jax.ShapeDtypeStruct((160, cells), BF),...]
    all_to_all x3 -> x0, blocking collectives: 85.6 us -> none  [the longest x2 54.5 us: analyse(): lax.all_to_all(projected, 'gy', split_axis=3, concat_axis=1, tiled=True)]
    dot_general x26 -> x0, matrix products: 44.6 us -> none  [the longest x4 10.6 us: split_product_first(): lax.dot_general(halves[1], right, dims, preferred_element_type=jnp.float32)]
    all_gather x2 -> x0, blocking collectives: 44.3 us -> none  [synthesise(): portion = lax.all_gather(coeffs, 'gz', axis=0, tiled=True)]
    convert_element_type x13 -> x0, local copies, waits for them, and re-layouts: 33.6 us -> none  [the longest x4 13.3 us: split_matrix(): low_part = (matrix - high_part.astype(jnp.float32)).astype(jnp.bfloat16)]
    reshape x23 -> x4, local copies, waits for them, and re-layouts: 37.5 us -> 9.02 us  [the longest x2 4.64 us: per_device(): return (layer.reshape(field.shape), fgrad.reshape(field.shape), wgrad)]
    all_to_all x10 -> x0, local copies, waits for them, and re-layouts: 24.8 us -> none  [the longest x6 16.3 us: analyse(): lax.all_to_all(projected, 'gy', split_axis=3, concat_axis=1, tiled=True)]
  transfers between devices with their start and end apart: 3 -> 0, of which waited for: 3 -> 0; matrix products, arithmetic and copies ran while one was open for 8% -> 0% of each run, Pallas kernels for 0% -> 0%
where the time goes in v1:
time: 122 us
  Pallas kernels  111 us (91%)
  local copies, waits for them, and re-layouts  10 us (8%)
    pallas_call x1, Pallas kernels, per_device(): pl.pallas_call(kernel, out_shape=(jax.ShapeDtypeStruct((160, cells), BF),...  111 us
    reshape x2, local copies, waits for them, and re-layouts, per_device(): return (layer.reshape(field.shape), fgrad.reshape(field.shape), wgrad)  4.64 us

profile of v1, /device:TPU:1, one launch (start us, length us, event | category | flops | bytes accessed | tf_op | source)
XLA Modules:
  0.0 121.9 jit_solution(4313888598806407812)
XLA Ops:
  0.6 2.2 %reshape.21.field_hbm = bf16[160,2048]{1,0:T(8,128)(2,1)} reshape(bf16[20,2,4,2048]{3,2,1,0:T(4,128)(2,1)} %param.13) | data formatting | bytes 1310720 | tf_op jit(solution)/shard_map/reshape | solution.py:411
  2.8 2.2 %reshape.22.cot_hbm = bf16[160,2048]{1,0:T(8,128)(2,1)} reshape(bf16[20,2,4,2048]{3,2,1,0:T(4,128)(2,1)} %param.14) | data formatting | bytes 1310720 | tf_op jit(solution)/shard_map/reshape | solution.py:412
  5.0 111.2 %shard_map.148 = (bf16[160,2048]{1,0:T(8,128)(2,1)}, bf16[160,2048]{1,0:T(8,128)(2,1)}, f32[36,7200]{1,0:T(8,128)}) custom-call(bf16[160,2048]{1,0:T(8,128)(2,1)} %reshape.21.field_hbm, bf16[160,2048]{1,0:T(8,128)(2,1)} %reshape.22.cot_hbm, bf16[36,7200]{1,0:T(8,128)(2,1)} %weight_hbm.1, bf16[20,20]{1,0:T(8,128)(2,1)} %point_ref.1, f32[1,20]{1,0:T(1,128)} %bitcast.1, ...), custom_call_target="tpu_custom_call" | custom-call | tf_op jit(solution)/shard_map/pallas_call | solution.py:457
  116.2 0.0 copy-start
  116.2 2.4 %reshape.24 = bf16[20,2,4,2048]{3,2,1,0:T(4,128)(2,1)} reshape(bf16[160,2048]{1,0:T(8,128)(2,1)} %get-tuple-element.6) | data formatting | bytes 1310720 | tf_op jit(solution)/shard_map/reshape | solution.py:471
  118.6 2.3 %reshape.25 = bf16[20,2,4,2048]{3,2,1,0:T(4,128)(2,1)} reshape(bf16[160,2048]{1,0:T(8,128)(2,1)} %get-tuple-element.7) | data formatting | bytes 1310720 | tf_op jit(solution)/shard_map/reshape | solution.py:471
  120.9 0.0 copy-done
  120.9 1.0 copy.17
Async XLA Ops:
  116.2 4.6 %copy-start = (f32[36,7200]{1,0:T(8,128)S(1)}, f32[36,7200]{1,0:T(8,128)}, u32[]{:S(2)}) copy-start(f32[36,7200]{1,0:T(8,128)} %get-tuple-element.14) | copy-start | bytes 3110404

commit v2 on v1

v2 whole, which is shorter than its diff:
```python
import functools

import jax
import jax.numpy as jnp
import ml_dtypes
import numpy as np
from jax import lax
from jax.experimental import pallas as pl
from jax.experimental.pallas import tpu as pltpu
from jax.sharding import PartitionSpec as P

MODES = 12
NX = 64
NY = 64
NZ = 64
NT = 32
CH = 20
GY = 32
GZ = 16
PAIRS = 36
PROWS = 40
SLAB = 8
PARTS = 3
LINES = 168
MESH = pl.DeviceIdType.MESH
BF = jnp.bfloat16
F32 = jnp.float32


def kept(slots, length):
    return np.where(slots < MODES, slots, length - 2 * MODES + slots)


def plane_constant():
    cell = np.arange(NX * NT)
    x, t = cell // NT, cell % NT
    out = np.zeros((GY, 3, 8, NX * NT))
    for d in range(GY):
        for k in range(3):
            for q3 in range(3):
                q = 9 * d + 3 * k + q3
                kx, kt = kept(np.array(q // MODES), NX), q % MODES
                angle = 2 * np.pi * ((kx * x % NX) / NX + (kt * t % NT) / NT)
                out[d, k, 2 * q3] = np.cos(angle)
                out[d, k, 2 * q3 + 1] = -np.sin(angle)
    return out.transpose(1, 0, 2, 3).reshape(PARTS, GY * SLAB, NX * NT)


def slot_frequency(length):
    g = np.arange(GZ)[:, None]
    return kept(3 * g // 2 + np.arange(2)[None, :], length)


def on_slabs(cosine, sine):
    rows, cols = cosine.shape
    two = np.stack([np.stack([cosine, sine], -1), np.stack([-sine, cosine], -1)], 2)
    full = np.einsum("rcab,uv->ruacvb", two.transpose(0, 1, 2, 3), np.eye(4))
    return full.reshape(rows * SLAB, cols * SLAB)


def y_constants():
    ky = slot_frequency(NY)
    y = 2 * np.arange(GY)[None, :] + np.arange(2)[:, None]
    angle = 2 * np.pi * (ky[None, :, :, None] * y[:, None, None, :] % NY) / NY
    near = angle.transpose(0, 2, 1, 3)
    forward = on_slabs(np.cos(near).reshape(-1, GY), np.sin(near).reshape(-1, GY))
    far = angle.transpose(0, 2, 3, 1)
    back = on_slabs(np.cos(far).reshape(-1, GZ), -np.sin(far).reshape(-1, GZ))
    return forward, back


def pair_slots(parity):
    p = np.arange(PAIRS) + 12 * parity
    return p // 24, p % 24


def z_constants():
    forward = np.zeros((2, 4, 2, LINES, GZ, 4, 2))
    back = np.zeros((2, 4, GZ, 4, 2, 2, LINES))
    for parity in range(2):
        kz = kept(pair_slots(parity)[1], NZ)
        for zl in range(4):
            angle = 2 * np.pi * (kz[:, None] * (4 * np.arange(GZ) + zl)[None, :] % NZ) / NZ
            c, s = np.cos(angle), np.sin(angle)
            for u in range(4):
                rows = slice(PROWS * u, PROWS * u + PAIRS) if u < 3 else slice(128, 128 + PAIRS)
                forward[parity, zl, 0, rows, :, u, 0] = c
                forward[parity, zl, 0, rows, :, u, 1] = s
                forward[parity, zl, 1, rows, :, u, 0] = -s
                forward[parity, zl, 1, rows, :, u, 1] = c
                back[parity, zl, :, u, 0, 0, rows] = c.T
                back[parity, zl, :, u, 0, 1, rows] = -s.T
                back[parity, zl, :, u, 1, 0, rows] = s.T
                back[parity, zl, :, u, 1, 1, rows] = c.T
    back = np.pad(back.reshape(2, 4 * GZ * SLAB, 2 * LINES), ((0, 0), (0, 0), (0, 384 - 2 * LINES)))
    return forward.reshape(2, 8 * LINES, GZ * SLAB), back


def mask_constant():
    lane = np.arange(128)
    out = np.zeros((2, 2, 128, 128))
    for parity in range(2):
        slot = pair_slots(parity)[0]
        for q3 in range(3):
            rows = slice(PROWS * q3, PROWS * q3 + PAIRS)
            match = (lane // 4 % 2)[None, :] == slot[:, None]
            out[parity, 0, rows] = match
            out[parity, 1, rows] = match & (lane // 32 == q3)[None, :]
    return out


def channel_constants():
    lane = np.arange(128)
    channel = np.concatenate([lane // 8, np.where(lane < 96, 16 + lane % 32 // 8, -1)])
    pair = np.arange(512)
    first = np.where(pair < CH * CH, pair // CH, -2)
    second = np.where(pair < CH * CH, pair % CH, -2)
    return channel[:, None] == first[None, :], channel[:, None] == second[None, :]


@functools.cache
def constants():
    half = lambda a: np.asarray(a, np.float32).astype(ml_dtypes.bfloat16)
    y_forward, y_back = y_constants()
    z_forward, z_back = z_constants()
    first, second = channel_constants()
    spread = np.stack([first, second])
    return (
        half(plane_constant()),
        half(y_forward),
        half(z_forward),
        half(z_back),
        half(y_back),
        half(spread),
        half(spread.transpose(0, 2, 1)),
        np.asarray(mask_constant(), np.float32),
    )


def dot(a, b):
    return jnp.dot(a, b, preferred_element_type=F32)


def dot_t(a, b):
    return lax.dot_general(a, b, (((1,), (1,)), ((), ())), preferred_element_type=F32)


def lanes(shape):
    return lax.broadcasted_iota(jnp.int32, shape, len(shape) - 1)


def kernel(
    field_hbm, cot_hbm, weight_hbm, point_ref, bias_ref,
    plane_hbm, yf_hbm, zf_hbm, zb_hbm, yb_hbm, spread_hbm, gather_hbm, mask_hbm,
    out_hbm, fgrad_hbm, wgrad_hbm,
    field, cot, weight, plane, yf, zf, zb, yb, spread, gather, mask,
    slope, layer, fgrad, wf, w0, w1, u0, u1, wg, wgrad, volume, turned, scale, point_fwd, point_bwd, bias_col,
    sy, ry, sz, rz, szb, rzb, syb, ryb, load_sem, store_sem, send_sem, recv_sem,
):
    j = lax.axis_index("gy")
    g = lax.axis_index("gz")
    parity = lax.rem(g, 2)

    def load(i, src, dst):
        copy = pltpu.make_async_copy(src, dst, load_sem.at[i])
        copy.start()
        return copy

    got_field = load(0, field_hbm, field.at[pl.ds(0, 160)])
    got_plane = [load(1 + k, plane_hbm.at[k], plane.at[k]) for k in range(PARTS)]
    got_yf = load(4, yf_hbm, yf)
    got_weight = load(5, weight_hbm, weight)
    got_zf = load(6, zf_hbm.at[parity], zf)
    got_spread = load(7, spread_hbm, spread)
    got_gather = load(8, gather_hbm, gather)
    got_mask = load(9, mask_hbm.at[parity], mask)
    got_zb = load(10, zb_hbm.at[parity], zb)
    got_yb = load(11, yb_hbm, yb)
    got_cot = load(12, cot_hbm, cot)

    barrier = pltpu.get_barrier_semaphore()

    def greet(axis, me, count):
        def one(k, carry):
            pl.semaphore_signal(barrier, inc=1, device_id={axis: lax.rem(me + k, count)}, device_id_type=MESH)
            return carry

        lax.fori_loop(1, count, one, 0)

    greet("gy", j, GY)
    greet("gz", g, GZ)

    def copy_to(src, dst, axis, me, other, which):
        pltpu.make_async_remote_copy(
            src_ref=src.at[other],
            dst_ref=dst.at[me],
            send_sem=send_sem.at[which],
            recv_sem=recv_sem.at[which],
            device_id={axis: other},
            device_id_type=MESH,
        ).start()

    def send_y(src, dst, which):
        near = j // 16 * 16
        far = 16 - near
        z = lax.rem(j, 16)
        half = lax.rem(z + 8, 16)
        copy_to(src, dst, "gy", j, near + half, which)
        copy_to(src, dst, "gy", j, far + half, which)

        def one(i, carry):
            up = lax.rem(z + 8 - i, 16)
            down = lax.rem(z + 8 + i, 16)
            copy_to(src, dst, "gy", j, far + up, which)
            copy_to(src, dst, "gy", j, far + down, which)
            copy_to(src, dst, "gy", j, near + up, which)
            copy_to(src, dst, "gy", j, near + down, which)
            return carry

        lax.fori_loop(1, 8, one, 0)
        copy_to(src, dst, "gy", j, far + z, which)
        dst[pl.ds(j, 1)] = src[pl.ds(j, 1)]

    def send_z(src, dst, which):
        def one(i, carry):
            copy_to(src, dst, "gz", g, lax.rem(g + 8 + i, 16), which)
            copy_to(src, dst, "gz", g, lax.rem(g + 8 - i, 16), which)
            return carry

        copy_to(src, dst, "gz", g, lax.rem(g + 8, 16), which)
        lax.fori_loop(1, 8, one, 0)
        dst[pl.ds(g, 1)] = src[pl.ds(g, 1)]

    def arrive(dst, count, which):
        part = pl.ds(0, count - 1)
        pltpu.make_async_copy(dst.at[part], dst.at[part], recv_sem.at[which]).wait()

    def sent(src, count, which):
        part = pl.ds(0, count - 1)
        pltpu.make_async_copy(src.at[part], src.at[part], send_sem.at[which]).wait()

    zlane = lanes((1, 128)) % 4
    low_slot = lanes((1, 128)) // 4 % 2 == 0
    row3 = lax.broadcasted_iota(jnp.int32, (1, 8, 128), 1)
    lane3 = lanes((1, 8, 128))

    def planes_out(source, k, buffer):
        full = dot_t(plane[k], source[...])
        main = full[:, :128].reshape(GY, 8, 128)
        left = full[:, 128:].reshape(GY, 8, 128)
        extra = jnp.zeros_like(main)
        for q3 in range(3):
            moved = pltpu.roll(left, 6 - 2 * q3, 1)
            if q3:
                moved = pltpu.roll(moved, 32 * q3, 2)
            extra = jnp.where(lane3 // 32 == q3, moved, extra)
        buffer[...] = jnp.where(row3 >= 6, extra, main).astype(BF)

    def planes_in(buffer, k):
        block = buffer[...].astype(F32)
        left = jnp.zeros_like(block)
        for q3 in range(3):
            moved = pltpu.roll(block, 2 + 2 * q3, 1)
            if q3:
                moved = pltpu.roll(moved, 128 - 32 * q3, 2)
            left = jnp.where(row3 // 2 == q3, moved, left)
        turned[k, 0:128] = block.reshape(256, 128).T.astype(BF)
        turned[k, 128:256] = left.reshape(256, 128).T.astype(BF)

    def swap_slots(same_low, same_high, cross_low, cross_high):
        crossed = jnp.where(low_slot, pltpu.roll(cross_low, 124, 1), pltpu.roll(cross_high, 4, 1))
        return jnp.where(low_slot, same_low, same_high) + crossed

    def y_forward(buffer, target):
        block = buffer[...].reshape(256, 128)
        part = [dot(yf[128 * n : 128 * n + 128], block) for n in range(4)]
        target[...] = swap_slots(part[0], part[3], part[2], part[1]).reshape(GZ, SLAB, 128).astype(BF)

    def y_back(buffer, target):
        block = buffer[...].reshape(128, 128)
        part = [dot(yb[256 * n : 256 * n + 256], block) for n in range(4)]
        target[...] = swap_slots(part[0], part[3], part[1], part[2]).reshape(GY, SLAB, 128).astype(BF)

    def by_z(parts):
        low = jnp.where(zlane == 0, parts[0], parts[1])
        high = jnp.where(zlane == 2, parts[2], parts[3])
        return jnp.where(zlane < 2, low, high)

    def z_forward(buffer, factor):
        block = buffer[...].reshape(128, 128)
        step = 2 * LINES
        values = by_z([dot(zf[step * n : step * n + step], block) for n in range(4)]).reshape(2, LINES, 128)
        left = values[:, 128:]
        left = jnp.concatenate([left, left, left, jnp.zeros((2, 8, 128), F32)], axis=1)
        main = values[:, :128] * mask[0:1]
        left = left * mask[1:2]
        if factor is not None:
            main, left = main * factor[None], left * factor[None]
        return jnp.concatenate([main.reshape(256, 128).astype(BF), left.reshape(256, 128).astype(BF)], axis=1)

    def z_back(mixed, n, factor, target):
        values = dot(mixed, gather[n])
        main = values[:, :128].reshape(2, 128, 128) * mask[0:1]
        left = values[:, 128:].reshape(2, 128, 128) * mask[1:2]
        if factor is not None:
            main, left = main * factor[None], left * factor[None]
        left = left[:, 0:40] + left[:, 40:80] + left[:, 80:120]
        rows = jnp.concatenate([main, left], axis=1).reshape(2 * LINES, 128)
        rows = jnp.concatenate([rows, jnp.zeros((384 - 2 * LINES, 128), F32)], axis=0).astype(BF)
        parts = [dot(zb[128 * n : 128 * n + 128], rows) for n in range(4)]
        target[...] = by_z(parts).reshape(GZ, SLAB, 128).astype(BF)

    def mix_forward(k):
        spread_u = dot(z_forward(rz.at[0, k], None), spread[0])
        real_u, imag_u = spread_u[:128], spread_u[128:]
        u0[k] = real_u
        u1[k] = imag_u
        mixed_real = (real_u * w0[k] - imag_u * w1[k]).astype(BF)
        mixed_imag = (real_u * w1[k] + imag_u * w0[k]).astype(BF)
        z_back(jnp.concatenate([mixed_real, mixed_imag], axis=0), 1, scale[k], szb.at[0, k])

    def mix_back(k):
        spread_g = dot(z_forward(rz.at[1, k], scale[k]), spread[1])
        real_g, imag_g = spread_g[:128], spread_g[128:]
        mixed_real = (real_g * w0[k] + imag_g * w1[k]).astype(BF)
        mixed_imag = (imag_g * w0[k] - real_g * w1[k]).astype(BF)
        z_back(jnp.concatenate([mixed_real, mixed_imag], axis=0), 0, None, szb.at[1, k])
        w0[k] = u0[k] * real_g + u1[k] * imag_g
        w1[k] = u0[k] * imag_g - u1[k] * real_g

    def align_weights():
        wf[...] = jnp.zeros((PROWS, 7296), F32)
        wf[0:PAIRS, 0:7200] = weight[...].astype(F32)
        w0[...] = jnp.zeros((PARTS, 128, 512), F32)
        w1[...] = jnp.zeros((PARTS, 128, 512), F32)
        for q in range(9):
            for part, held in enumerate((w0, w1)):
                start = 800 * q + 400 * part
                first, shift = start // 128 * 128, start % 128
                piece = wf[:, first : first + 512]
                if shift:
                    piece = pltpu.roll(piece, 512 - shift, 1)
                top = PROWS * (q % 3)
                held[q // 3, top : top + PROWS] = piece

    def return_weights():
        wg[...] = jnp.zeros((PROWS, 7296), F32)
        for q in range(9):
            for part, held in enumerate((w0, w1)):
                start = 800 * q + 400 * part
                first, shift = start // 128 * 128, start % 128
                top = PROWS * (q % 3)
                piece = held[q // 3, top : top + PROWS]
                if shift:
                    piece = pltpu.roll(piece, shift, 1)
                wg[:, first : first + 512] = wg[:, first : first + 512] + piece
        wgrad[...] = wg[0:PAIRS, 0:7200]

    def small_tables():
        row = lax.broadcasted_iota(jnp.int32, (128, 128), 0)
        for k in range(PARTS):
            mode = 9 * j + 3 * k + (row >= 40).astype(jnp.int32) + (row >= 80).astype(jnp.int32)
            scale[k] = jnp.where(mode % MODES == 0, 1.0, 2.0) * (1.0 / (NX * NY * NZ * NT))
        copies = (lax.broadcasted_iota(jnp.int32, (160, CH), 0) // 8 == lanes((160, CH))).astype(F32)
        copies_half = copies.astype(BF)
        same_row = lax.broadcasted_iota(jnp.int32, (160, 160), 0) % 8 == lanes((160, 160)) % 8
        by_out = dot_t(copies_half, point_ref[...]).astype(BF)
        by_in = dot(copies_half, point_ref[...]).astype(BF)
        point_fwd[...] = jnp.where(same_row, dot_t(by_out, copies_half), 0.0).astype(BF)
        point_bwd[...] = jnp.where(same_row, dot_t(by_in, copies_half), 0.0).astype(BF)
        bias_col[...] = jnp.broadcast_to(jnp.sum(copies * bias_ref[...], axis=1, keepdims=True), (160, 128))

    def each_chunk(step):
        def one(n, carry):
            step(pl.ds(pl.multiple_of(n * 256, 256), 256))
            return carry

        lax.fori_loop(0, NX * NT // 256, one, 0)

    def point_forward(cells):
        volume[:, cells] = dot(point_fwd[...], field[0:160, cells]) + bias_col[:, 0:1]

    def point_back(cells):
        volume[:, cells] = dot(point_bwd[...], slope[0:160, cells])

    def summed(k, cells):
        return volume[:, cells] + dot(turned[k, 0:160], plane[k, :, cells])

    def add_part(k):
        def step(cells):
            volume[:, cells] = summed(k, cells)

        planes_in(ryb.at[now[0], k], k)
        each_chunk(step)

    def activate(cells):
        preact = summed(2, cells)
        normal = 0.5 * (1.0 + lax.erf(preact * 0.7071067811865476))
        density = jnp.exp(-0.5 * preact * preact) * 0.3989422804014327
        layer[:, cells] = (preact * normal).astype(BF)
        slope[0:160, cells] = (cot[:, cells].astype(F32) * (normal + preact * density)).astype(BF)

    def finish(cells):
        fgrad[:, cells] = summed(2, cells).astype(BF)

    now = [0]

    def start_part(source, k):
        t = now[0]
        planes_out(source, k, sy.at[t, k])
        if t == 0 and k == 0:
            pl.semaphore_wait(barrier, GY + GZ - 2)
        send_y(sy.at[t, k], ry.at[t, k], 12 * t + k)

    def y_part(k):
        t = now[0]
        arrive(ry.at[t, k], GY, 12 * t + k)
        y_forward(ry.at[t, k], sz.at[t, k])
        send_z(sz.at[t, k], rz.at[t, k], 12 * t + 3 + k)

    def z_part(k):
        t = now[0]
        arrive(rz.at[t, k], GZ, 12 * t + 3 + k)
        if t == 0:
            mix_forward(k)
        else:
            mix_back(k)
        send_z(szb.at[t, k], rzb.at[t, k], 12 * t + 6 + k)

    def back_part(k):
        t = now[0]
        arrive(rzb.at[t, k], GZ, 12 * t + 6 + k)
        y_back(rzb.at[t, k], syb.at[t, k])
        send_y(syb.at[t, k], ryb.at[t, k], 12 * t + 9 + k)

    def end_part(k):
        arrive(ryb.at[now[0], k], GY, 12 * now[0] + 9 + k)

    field[160:256] = jnp.zeros((96, NX * NT), BF)
    slope[160:256] = jnp.zeros((96, NX * NT), BF)
    got_field.wait()
    for k in range(PARTS):
        got_plane[k].wait()
        start_part(field, k)
    got_weight.wait()
    align_weights()
    small_tables()
    each_chunk(point_forward)
    got_yf.wait()
    y_part(0)
    got_zf.wait()
    got_spread.wait()
    got_gather.wait()
    got_mask.wait()
    got_zb.wait()
    got_yb.wait()
    got_cot.wait()
    y_part(1)
    z_part(0)
    y_part(2)
    z_part(1)
    back_part(0)
    z_part(2)
    back_part(1)
    back_part(2)
    for k in range(2):
        end_part(k)
        add_part(k)
    end_part(2)
    planes_in(ryb.at[0, 2], 2)
    each_chunk(activate)
    put_layer = pltpu.make_async_copy(layer, out_hbm, store_sem.at[0])
    now[0] = 1
    for k in range(PARTS):
        start_part(slope, k)
    put_layer.start()
    each_chunk(point_back)
    y_part(0)
    y_part(1)
    z_part(0)
    y_part(2)
    z_part(1)
    back_part(0)
    z_part(2)
    back_part(1)
    back_part(2)
    return_weights()
    put_wgrad = pltpu.make_async_copy(wgrad, wgrad_hbm, store_sem.at[1])
    put_wgrad.start()
    for k in range(2):
        end_part(k)
        add_part(k)
    end_part(2)
    planes_in(ryb.at[1, 2], 2)
    each_chunk(finish)
    put_fgrad = pltpu.make_async_copy(fgrad, fgrad_hbm, store_sem.at[2])
    put_fgrad.start()
    for t in range(2):
        for k in range(PARTS):
            sent(sy.at[t, k], GY, 12 * t + k)
            sent(sz.at[t, k], GZ, 12 * t + 3 + k)
            sent(szb.at[t, k], GZ, 12 * t + 6 + k)
            sent(syb.at[t, k], GY, 12 * t + 9 + k)
    put_layer.wait()
    put_wgrad.wait()
    put_fgrad.wait()


def per_device(field, cotangent, spectral_weight, point_weight, channel_bias):
    cells = NX * NT
    flat = field.reshape(160, cells)
    flat_cot = cotangent.reshape(160, cells)
    whole = pl.BlockSpec(memory_space=pltpu.VMEM)
    anywhere = pl.BlockSpec(memory_space=pl.ANY)
    consts = constants()
    vm = pltpu.VMEM
    scratch = [
        vm((256, cells), BF),
        vm((160, cells), BF),
        vm((PAIRS, 7200), BF),
        vm((PARTS, 256, cells), BF),
        vm((512, 256), BF),
        vm((8 * LINES, 128), BF),
        vm((512, 384), BF),
        vm((1024, 128), BF),
        vm((2, 256, 512), BF),
        vm((2, 512, 256), BF),
        vm((2, 128, 128), F32),
        vm((256, cells), BF),
        vm((160, cells), BF),
        vm((160, cells), BF),
        vm((PROWS, 7296), F32),
        vm((PARTS, 128, 512), F32),
        vm((PARTS, 128, 512), F32),
        vm((PARTS, 128, 512), F32),
        vm((PARTS, 128, 512), F32),
        vm((PROWS, 7296), F32),
        vm((PAIRS, 7200), F32),
        vm((160, cells), F32),
        vm((PARTS, 256, 256), BF),
        vm((PARTS, 128, 128), F32),
        vm((160, 160), BF),
        vm((160, 160), BF),
        vm((160, 128), F32),
        vm((2, PARTS, GY, SLAB, 128), BF),
        vm((2, PARTS, GY, SLAB, 128), BF),
        vm((2, PARTS, GZ, SLAB, 128), BF),
        vm((2, PARTS, GZ, SLAB, 128), BF),
        vm((2, PARTS, GZ, SLAB, 128), BF),
        vm((2, PARTS, GZ, SLAB, 128), BF),
        vm((2, PARTS, GY, SLAB, 128), BF),
        vm((2, PARTS, GY, SLAB, 128), BF),
        pltpu.SemaphoreType.DMA((13,)),
        pltpu.SemaphoreType.DMA((3,)),
        pltpu.SemaphoreType.DMA((24,)),
        pltpu.SemaphoreType.DMA((24,)),
    ]
    layer, fgrad, wgrad = pl.pallas_call(
        kernel,
        out_shape=(
            jax.ShapeDtypeStruct((160, cells), BF),
            jax.ShapeDtypeStruct((160, cells), BF),
            jax.ShapeDtypeStruct((PAIRS, 7200), F32),
        ),
        in_specs=[anywhere, anywhere, anywhere, whole, whole] + [anywhere] * len(consts),
        out_specs=(anywhere, anywhere, anywhere),
        scratch_shapes=scratch,
        compiler_params=pltpu.CompilerParams(
            collective_id=0, has_side_effects=True, vmem_limit_bytes=60 * 1024 * 1024
        ),
    )(flat, flat_cot, spectral_weight, point_weight, channel_bias.reshape(1, CH), *consts)
    return layer.reshape(field.shape), fgrad.reshape(field.shape), wgrad


def solution(mesh):
    return jax.shard_map(
        per_device,
        mesh=mesh,
        in_specs=(P(None, "gy", "gz", None), P(None, "gy", "gz", None), P("gz", "gy"), P(), P()),
        out_specs=(P(None, "gy", "gz", None), P(None, "gy", "gz", None), P("gz", "gy")),
        check_vma=False,
    )
```

time: 122 us -> 97.4 us (0.80)
  Pallas kernels: 111 us -> 88.8 us
  local copies, waits for them, and re-layouts: 10 us -> 7.75 us
    pallas_call x1, Pallas kernels: 111 us -> 88.8 us  [per_device(): pl.pallas_call(kernel, out_shape=(jax.ShapeDtypeStruct((160, cells), BF),...]
where the time goes in v2:
time: 97.4 us; the launch traced here: 97.2 us
  Pallas kernels  88.8 us (91%)
  local copies, waits for them, and re-layouts  7.75 us (8%)
    pallas_call x1, Pallas kernels, per_device(): pl.pallas_call(kernel, out_shape=(jax.ShapeDtypeStruct((160, cells), BF),...  88.8 us
    reshape x2, local copies, waits for them, and re-layouts, per_device(): return (layer.reshape(field.shape), fgrad.reshape(field.shape), wgrad)  3.48 us
    reshape x1, local copies, waits for them, and re-layouts, per_device(): flat = field.reshape(160, cells)  2.26 us

profile of v2, /device:TPU:1, one launch (start us, length us, event | category | flops | bytes accessed | tf_op | source)
XLA Modules:
  0.0 97.2 jit_solution(10032460585369104301)
XLA Ops:
  0.6 0.0 copy-start.1
  0.6 2.3 %reshape.21.field_hbm = bf16[160,2048]{1,0:T(8,128)(2,1)} reshape(bf16[20,2,4,2048]{3,2,1,0:T(4,128)(2,1)} %param.13) | data formatting | bytes 1310720 | tf_op jit(solution)/shard_map/reshape | solution.py:511
  2.9 0.0 copy-done.1
  2.9 1.0 %reshape.22.cot_hbm = bf16[160,2048]{1,0:T(8,128)(2,1)} reshape(bf16[20,2,4,2048]{3,2,1,0:T(4,128)(2,1)S(1)} %copy-done.1) | data formatting | bytes 1310720 | tf_op jit(solution)/shard_map/reshape | solution.py:512
  3.9 88.8 %shard_map.148 = (bf16[160,2048]{1,0:T(8,128)(2,1)}, bf16[160,2048]{1,0:T(8,128)(2,1)}, f32[36,7200]{1,0:T(8,128)}) custom-call(bf16[160,2048]{1,0:T(8,128)(2,1)} %reshape.21.field_hbm, bf16[160,2048]{1,0:T(8,128)(2,1)} %reshape.22.cot_hbm, bf16[36,7200]{1,0:T(8,128)(2,1)} %weight_hbm.1, bf16[20,20]{1,0:T(8,128)(2,1)} %point_ref.1, f32[1,20]{1,0:T(1,128)} %bitcast.1, ...), custom_call_target="tpu_custom_call" | custom-call | tf_op jit(solution)/shard_map/pallas_call | solution.py:558
  92.7 0.0 copy-start.2
  92.7 0.0 copy-start
  92.7 2.4 %reshape.24 = bf16[20,2,4,2048]{3,2,1,0:T(4,128)(2,1)} reshape(bf16[160,2048]{1,0:T(8,128)(2,1)} %get-tuple-element.6) | data formatting | bytes 1310720 | tf_op jit(solution)/shard_map/reshape | solution.py:572
  95.1 0.0 copy-done.2
  95.1 1.1 %reshape.25 = bf16[20,2,4,2048]{3,2,1,0:T(4,128)(2,1)} reshape(bf16[160,2048]{1,0:T(8,128)(2,1)S(1)} %copy-done.2) | data formatting | bytes 1310720 | tf_op jit(solution)/shard_map/reshape | solution.py:572
  96.2 0.0 copy-done
  96.2 1.0 %copy.17 = f32[36,7200]{1,0:T(8,128)} copy(f32[36,7200]{1,0:T(8,128)S(1)} %copy-done) | data formatting | bytes 2073600
Async XLA Ops:
  0.6 2.3 %copy-start.1 = (bf16[20,2,4,2048]{3,2,1,0:T(4,128)(2,1)S(1)}, bf16[20,2,4,2048]{3,2,1,0:T(4,128)(2,1)}, u32[]{:S(2)}) copy-start(bf16[20,2,4,2048]{3,2,1,0:T(4,128)(2,1)} %param.14) | copy-start | bytes 1966084
  92.7 2.4 %copy-start.2 = (bf16[160,2048]{1,0:T(8,128)(2,1)S(1)}, bf16[160,2048]{1,0:T(8,128)(2,1)}, u32[]{:S(2)}) copy-start(bf16[160,2048]{1,0:T(8,128)(2,1)} %get-tuple-element.7) | copy-start | bytes 1966084
  92.7 3.5 %copy-start = (f32[36,7200]{1,0:T(8,128)S(1)}, f32[36,7200]{1,0:T(8,128)}, u32[]{:S(2)}) copy-start(f32[36,7200]{1,0:T(8,128)} %get-tuple-element.14) | copy-start | bytes 3110404

commit v3 on v2

--- a/solution.py
+++ b/solution.py
@@ -154,19 +154,55 @@
     plane_hbm, yf_hbm, zf_hbm, zb_hbm, yb_hbm, spread_hbm, gather_hbm, mask_hbm,
     out_hbm, fgrad_hbm, wgrad_hbm,
     field, cot, weight, plane, yf, zf, zb, yb, spread, gather, mask,
-    slope, layer, fgrad, wf, w0, w1, u0, u1, wg, wgrad, volume, turned, scale, point_fwd, point_bwd, bias_col,
+    slope, layer, wf, w0, w1, u0, u1, wg, wgrad, volume, turned, scale, point_fwd, point_bwd, bias_col,
+    field_raw, cot_raw, layer_raw, fgrad_raw,
     sy, ry, sz, rz, szb, rzb, syb, ryb, load_sem, store_sem, send_sem, recv_sem,
 ):
     j = lax.axis_index("gy")
     g = lax.axis_index("gz")
     parity = lax.rem(g, 2)
 
+    barrier = pltpu.get_barrier_semaphore()
+
+    def greet(axis, other):
+        pl.semaphore_signal(barrier, inc=1, device_id={axis: other}, device_id_type=MESH)
+
+    def greet_y():
+        near = j // 16 * 16
+        far = 16 - near
+        z = lax.rem(j, 16)
+        half = lax.rem(z + 8, 16)
+        greet("gy", far + half)
+        greet("gy", near + half)
+
+        def one(i, carry):
+            up = lax.rem(z + 8 - i, 16)
+            down = lax.rem(z + 8 + i, 16)
+            greet("gy", far + up)
+            greet("gy", far + down)
+            greet("gy", near + up)
+            greet("gy", near + down)
+            return carry
+
+        lax.fori_loop(1, 8, one, 0)
+        greet("gy", far + z)
+
+    def greet_z():
+        def one(i, carry):
+            greet("gz", lax.rem(g + i, 16))
+            return carry
+
+        lax.fori_loop(1, 16, one, 0)
+
+    greet_y()
+    greet_z()
+
     def load(i, src, dst):
         copy = pltpu.make_async_copy(src, dst, load_sem.at[i])
         copy.start()
         return copy
 
-    got_field = load(0, field_hbm, field.at[pl.ds(0, 160)])
+    got_field = load(0, field_hbm, field_raw)
     got_plane = [load(1 + k, plane_hbm.at[k], plane.at[k]) for k in range(PARTS)]
     got_yf = load(4, yf_hbm, yf)
     got_weight = load(5, weight_hbm, weight)
@@ -176,19 +212,7 @@
     got_mask = load(9, mask_hbm.at[parity], mask)
     got_zb = load(10, zb_hbm.at[parity], zb)
     got_yb = load(11, yb_hbm, yb)
-    got_cot = load(12, cot_hbm, cot)
-
-    barrier = pltpu.get_barrier_semaphore()
-
-    def greet(axis, me, count):
-        def one(k, carry):
-            pl.semaphore_signal(barrier, inc=1, device_id={axis: lax.rem(me + k, count)}, device_id_type=MESH)
-            return carry
-
-        lax.fori_loop(1, count, one, 0)
-
-    greet("gy", j, GY)
-    greet("gz", g, GZ)
+    got_cot = load(12, cot_hbm, cot_raw)
 
     def copy_to(src, dst, axis, me, other, which):
         pltpu.make_async_remote_copy(
@@ -401,16 +425,24 @@
         slope[0:160, cells] = (cot[:, cells].astype(F32) * (normal + preact * density)).astype(BF)
 
     def finish(cells):
-        fgrad[:, cells] = summed(2, cells).astype(BF)
+        fgrad_raw[:, :, :, cells] = summed(2, cells).reshape(CH, 2, 4, 256).astype(BF)
+        pltpu.make_async_copy(
+            fgrad_raw.at[:, :, :, cells], fgrad_hbm.at[:, :, :, cells], store_sem.at[2]
+        ).start()
+
+    def flatten(raw, flat):
+        flat[0:160] = raw[...].astype(F32).reshape(160, NX * NT).astype(BF)
+
+    def unflatten(flat, raw):
+        raw[...] = flat[...].astype(F32).reshape(CH, 2, 4, NX * NT).astype(BF)
 
     now = [0]
 
     def start_part(source, k):
         t = now[0]
         planes_out(source, k, sy.at[t, k])
-        if t == 0 and k == 0:
-            pl.semaphore_wait(barrier, GY + GZ - 2)
-        send_y(sy.at[t, k], ry.at[t, k], 12 * t + k)
+        if t == 1:
+            send_y(sy.at[t, k], ry.at[t, k], 12 * t + k)
 
     def y_part(k):
         t = now[0]
@@ -439,9 +471,13 @@
     field[160:256] = jnp.zeros((96, NX * NT), BF)
     slope[160:256] = jnp.zeros((96, NX * NT), BF)
     got_field.wait()
+    flatten(field_raw, field)
     for k in range(PARTS):
         got_plane[k].wait()
         start_part(field, k)
+    pl.semaphore_wait(barrier, GY + GZ - 2)
+    for k in range(PARTS):
+        send_y(sy.at[0, k], ry.at[0, k], k)
     got_weight.wait()
     align_weights()
     small_tables()
@@ -455,9 +491,10 @@
     got_zb.wait()
     got_yb.wait()
     got_cot.wait()
+    flatten(cot_raw, cot)
     y_part(1)
+    y_part(2)
     z_part(0)
-    y_part(2)
     z_part(1)
     back_part(0)
     z_part(2)
@@ -469,16 +506,17 @@
     end_part(2)
     planes_in(ryb.at[0, 2], 2)
     each_chunk(activate)
-    put_layer = pltpu.make_async_copy(layer, out_hbm, store_sem.at[0])
+    put_layer = pltpu.make_async_copy(layer_raw, out_hbm, store_sem.at[0])
     now[0] = 1
     for k in range(PARTS):
         start_part(slope, k)
+    unflatten(layer, layer_raw)
     put_layer.start()
     each_chunk(point_back)
     y_part(0)
     y_part(1)
+    y_part(2)
     z_part(0)
-    y_part(2)
     z_part(1)
     back_part(0)
     z_part(2)
@@ -493,8 +531,6 @@
     end_part(2)
     planes_in(ryb.at[1, 2], 2)
     each_chunk(finish)
-    put_fgrad = pltpu.make_async_copy(fgrad, fgrad_hbm, store_sem.at[2])
-    put_fgrad.start()
     for t in range(2):
         for k in range(PARTS):
             sent(sy.at[t, k], GY, 12 * t + k)
@@ -503,13 +539,11 @@
             sent(syb.at[t, k], GY, 12 * t + 9 + k)
     put_layer.wait()
     put_wgrad.wait()
-    put_fgrad.wait()
+    pltpu.make_async_copy(fgrad_raw, fgrad_hbm, store_sem.at[2]).wait()
 
 
 def per_device(field, cotangent, spectral_weight, point_weight, channel_bias):
     cells = NX * NT
-    flat = field.reshape(160, cells)
-    flat_cot = cotangent.reshape(160, cells)
     whole = pl.BlockSpec(memory_space=pltpu.VMEM)
     anywhere = pl.BlockSpec(memory_space=pl.ANY)
     consts = constants()
@@ -528,7 +562,6 @@
         vm((2, 128, 128), F32),
         vm((256, cells), BF),
         vm((160, cells), BF),
-        vm((160, cells), BF),
         vm((PROWS, 7296), F32),
         vm((PARTS, 128, 512), F32),
         vm((PARTS, 128, 512), F32),
@@ -542,6 +575,10 @@
         vm((160, 160), BF),
         vm((160, 160), BF),
         vm((160, 128), F32),
+        vm((CH, 2, 4, cells), BF),
+        vm((CH, 2, 4, cells), BF),
+        vm((CH, 2, 4, cells), BF),
+        vm((CH, 2, 4, cells), BF),
         vm((2, PARTS, GY, SLAB, 128), BF),
         vm((2, PARTS, GY, SLAB, 128), BF),
         vm((2, PARTS, GZ, SLAB, 128), BF),
@@ -558,8 +595,8 @@
     layer, fgrad, wgrad = pl.pallas_call(
         kernel,
         out_shape=(
-            jax.ShapeDtypeStruct((160, cells), BF),
-            jax.ShapeDtypeStruct((160, cells), BF),
+            jax.ShapeDtypeStruct(field.shape, BF),
+            jax.ShapeDtypeStruct(field.shape, BF),
             jax.ShapeDtypeStruct((PAIRS, 7200), F32),
         ),
         in_specs=[anywhere, anywhere, anywhere, whole, whole] + [anywhere] * len(consts),
@@ -568,8 +605,8 @@
         compiler_params=pltpu.CompilerParams(
             collective_id=0, has_side_effects=True, vmem_limit_bytes=60 * 1024 * 1024
         ),
-    )(flat, flat_cot, spectral_weight, point_weight, channel_bias.reshape(1, CH), *consts)
-    return layer.reshape(field.shape), fgrad.reshape(field.shape), wgrad
+    )(field, cotangent, spectral_weight, point_weight, channel_bias.reshape(1, CH), *consts)
+    return layer, fgrad, wgrad
 
 
 def solution(mesh):

time: 97.4 us -> 95.3 us (0.978)
  local copies, waits for them, and re-layouts: 7.75 us -> 4.25 us
  Pallas kernels: 88.8 us -> 90.2 us
    reshape x4 -> x0, local copies, waits for them, and re-layouts: 6.73 us -> none  [the longest x2 3.48 us: per_device(): return (layer.reshape(field.shape), fgrad.reshape(field.shape), wgrad)]
    unnamed x7, local copies, waits for them, and re-layouts: 1.02 us -> 4.25 us
    pallas_call x1, Pallas kernels: 88.8 us -> 90.2 us  [per_device(): pl.pallas_call(kernel, out_shape=(jax.ShapeDtypeStruct(field.shape, BF),...]
where the time goes in v3:
time: 95.3 us; the launch traced here: 95.1 us
  Pallas kernels  90.2 us (95%)
  local copies, waits for them, and re-layouts  4.25 us (4%)
    pallas_call x1, Pallas kernels, per_device(): pl.pallas_call(kernel, out_shape=(jax.ShapeDtypeStruct(field.shape, BF),...  90.2 us
    unnamed x7, local copies, waits for them, and re-layouts  4.25 us

profile of v3, /device:TPU:1, one launch (start us, length us, event | category | flops | bytes accessed | tf_op | source)
XLA Modules:
  0.0 95.1 jit_solution(999234988054730434)
XLA Ops:
  0.6 90.2 %shard_map.148 = (bf16[20,2,4,2048]{3,2,1,0:T(4,128)(2,1)}, bf16[20,2,4,2048]{3,2,1,0:T(4,128)(2,1)}, f32[36,7200]{1,0:T(8,128)}) custom-call(bf16[20,2,4,2048]{3,2,1,0:T(4,128)(2,1)} %field_hbm.1, bf16[20,2,4,2048]{3,2,1,0:T(4,128)(2,1)} %cot_hbm.1, bf16[36,7200]{1,0:T(8,128)(2,1)} %weight_hbm.1, bf16[20,20]{1,0:T(8,128)(2,1)} %point_ref.1, ...), custom_call_target="tpu_custom_call" | custom-call | tf_op jit(solution)/shard_map/pallas_call | solution.py:595
  90.9 0.0 copy-start.1
  90.9 0.0 copy-start
  90.9 2.4 %copy.19 = bf16[20,2,4,2048]{3,2,1,0:T(4,128)(2,1)} copy(bf16[20,2,4,2048]{3,2,1,0:T(4,128)(2,1)} %get-tuple-element.6) | data formatting | bytes 1310720
  93.3 0.0 copy-done.1
  93.3 0.8 copy.20
  94.1 0.0 copy-done
  94.1 1.0 %copy.21 = f32[36,7200]{1,0:T(8,128)} copy(f32[36,7200]{1,0:T(8,128)S(1)} %copy-done) | data formatting | bytes 2073600
Async XLA Ops:
  90.9 2.4 %copy-start.1 = (bf16[20,2,4,2048]{3,2,1,0:T(4,128)(2,1)S(1)}, bf16[20,2,4,2048]{3,2,1,0:T(4,128)(2,1)}, u32[]{:S(2)}) copy-start(bf16[20,2,4,2048]{3,2,1,0:T(4,128)(2,1)} %get-tuple-element.7) | copy-start | bytes 1966084
  90.9 3.3 %copy-start = (f32[36,7200]{1,0:T(8,128)S(1)}, f32[36,7200]{1,0:T(8,128)}, u32[]{:S(2)}) copy-start(f32[36,7200]{1,0:T(8,128)} %get-tuple-element.8) | copy-start | bytes 3110404

commit v4 on v3

--- a/solution.py
+++ b/solution.py
@@ -246,13 +246,8 @@
         dst[pl.ds(j, 1)] = src[pl.ds(j, 1)]
 
     def send_z(src, dst, which):
-        def one(i, carry):
-            copy_to(src, dst, "gz", g, lax.rem(g + 8 + i, 16), which)
-            copy_to(src, dst, "gz", g, lax.rem(g + 8 - i, 16), which)
-            return carry
-
-        copy_to(src, dst, "gz", g, lax.rem(g + 8, 16), which)
-        lax.fori_loop(1, 8, one, 0)
+        for step in (12, 13, 11, 10, 14, 8, 9, 15, 4, 5, 3, 2, 6, 7, 1):
+            copy_to(src, dst, "gz", g, lax.rem(g + step, 16), which)
         dst[pl.ds(g, 1)] = src[pl.ds(g, 1)]
 
     def arrive(dst, count, which):
@@ -289,7 +284,7 @@
                 moved = pltpu.roll(moved, 128 - 32 * q3, 2)
             left = jnp.where(row3 // 2 == q3, moved, left)
         turned[k, 0:128] = block.reshape(256, 128).T.astype(BF)
-        turned[k, 128:256] = left.reshape(256, 128).T.astype(BF)
+        turned[k, 128:160] = left.reshape(256, 128)[:, 0:32].T.astype(BF)
 
     def swap_slots(same_low, same_high, cross_low, cross_high):
         crossed = jnp.where(low_slot, pltpu.roll(cross_low, 124, 1), pltpu.roll(cross_high, 4, 1))
@@ -297,12 +292,14 @@
 
     def y_forward(buffer, target):
         block = buffer[...].reshape(256, 128)
-        part = [dot(yf[128 * n : 128 * n + 128], block) for n in range(4)]
+        every = dot(yf[...], block)
+        part = [every[128 * n : 128 * n + 128] for n in range(4)]
         target[...] = swap_slots(part[0], part[3], part[2], part[1]).reshape(GZ, SLAB, 128).astype(BF)
 
     def y_back(buffer, target):
         block = buffer[...].reshape(128, 128)
-        part = [dot(yb[256 * n : 256 * n + 256], block) for n in range(4)]
+        every = dot(yb[...], block)
+        part = [every[256 * n : 256 * n + 256] for n in range(4)]
         target[...] = swap_slots(part[0], part[3], part[1], part[2]).reshape(GY, SLAB, 128).astype(BF)
 
     def by_z(parts):
@@ -313,7 +310,8 @@
     def z_forward(buffer, factor):
         block = buffer[...].reshape(128, 128)
         step = 2 * LINES
-        values = by_z([dot(zf[step * n : step * n + step], block) for n in range(4)]).reshape(2, LINES, 128)
+        every = dot(zf[...], block)
+        values = by_z([every[step * n : step * n + step] for n in range(4)]).reshape(2, LINES, 128)
         left = values[:, 128:]
         left = jnp.concatenate([left, left, left, jnp.zeros((2, 8, 128), F32)], axis=1)
         main = values[:, :128] * mask[0:1]
@@ -331,7 +329,8 @@
         left = left[:, 0:40] + left[:, 40:80] + left[:, 80:120]
         rows = jnp.concatenate([main, left], axis=1).reshape(2 * LINES, 128)
         rows = jnp.concatenate([rows, jnp.zeros((384 - 2 * LINES, 128), F32)], axis=0).astype(BF)
-        parts = [dot(zb[128 * n : 128 * n + 128], rows) for n in range(4)]
+        every = dot(zb[...], rows)
+        parts = [every[128 * n : 128 * n + 128] for n in range(4)]
         target[...] = by_z(parts).reshape(GZ, SLAB, 128).astype(BF)
 
     def mix_forward(k):
@@ -415,7 +414,8 @@
             volume[:, cells] = summed(k, cells)
 
         planes_in(ryb.at[now[0], k], k)
-        each_chunk(step)
+        for n in range(8):
+            step(pl.ds(256 * n, 256))
 
     def activate(cells):
         preact = summed(2, cells)
@@ -505,7 +505,8 @@
         add_part(k)
     end_part(2)
     planes_in(ryb.at[0, 2], 2)
-    each_chunk(activate)
+    for n in range(8):
+        activate(pl.ds(256 * n, 256))
     put_layer = pltpu.make_async_copy(layer_raw, out_hbm, store_sem.at[0])
     now[0] = 1
     for k in range(PARTS):
@@ -525,21 +526,56 @@
     return_weights()
     put_wgrad = pltpu.make_async_copy(wgrad, wgrad_hbm, store_sem.at[1])
     put_wgrad.start()
+    for t in range(2):
+        for k in range(PARTS):
+            sent(sy.at[t, k], GY, 12 * t + k)
+            sent(sz.at[t, k], GZ, 12 * t + 3 + k)
+            sent(szb.at[t, k], GZ, 12 * t + 6 + k)
+            if t == 0:
+                sent(syb.at[t, k], GY, 12 * t + 9 + k)
+    put_layer.wait()
+    put_wgrad.wait()
     for k in range(2):
         end_part(k)
         add_part(k)
     end_part(2)
     planes_in(ryb.at[1, 2], 2)
-    each_chunk(finish)
-    for t in range(2):
-        for k in range(PARTS):
-            sent(sy.at[t, k], GY, 12 * t + k)
-            sent(sz.at[t, k], GZ, 12 * t + 3 + k)
-            sent(szb.at[t, k], GZ, 12 * t + 6 + k)
-            sent(syb.at[t, k], GY, 12 * t + 9 + k)
-    put_layer.wait()
-    put_wgrad.wait()
+    for n in range(8):
+        finish(pl.ds(256 * n, 256))
+    for k in range(PARTS):
+        sent(syb.at[1, k], GY, 21 + k)
     pltpu.make_async_copy(fgrad_raw, fgrad_hbm, store_sem.at[2]).wait()
+
+
+def store_kernel(*refs):
+    sources, targets, held, sem_in, sem_out = refs[:3], refs[3:6], refs[6:9], refs[9], refs[10]
+    arriving, leaving = [], []
+    for source, target, room in zip(sources, targets, held):
+        pieces = [(4 * n, 4) for n in range(5)] if len(source.shape) == 4 else [(0, 8), (8, 8), (16, 8), (24, 12)]
+        for first, count in pieces:
+            rows = pl.ds(first, count)
+            n = len(arriving)
+            copy = pltpu.make_async_copy(source.at[rows], room.at[rows], sem_in.at[n])
+            copy.start()
+            arriving.append(copy)
+            leaving.append(pltpu.make_async_copy(room.at[rows], target.at[rows], sem_out.at[n]))
+    for copy, after in zip(arriving, leaving):
+        copy.wait()
+        after.start()
+    for after in leaving:
+        after.wait()
+
+
+def store(*arrays):
+    anywhere = pl.BlockSpec(memory_space=pl.ANY)
+    return pl.pallas_call(
+        store_kernel,
+        out_shape=tuple(jax.ShapeDtypeStruct(a.shape, a.dtype) for a in arrays),
+        in_specs=[anywhere] * 3,
+        out_specs=(anywhere,) * 3,
+        scratch_shapes=[pltpu.VMEM(a.shape, a.dtype) for a in arrays] + [pltpu.SemaphoreType.DMA((14,))] * 2,
+        compiler_params=pltpu.CompilerParams(vmem_limit_bytes=60 * 1024 * 1024),
+    )(*arrays)
 
 
 def per_device(field, cotangent, spectral_weight, point_weight, channel_bias):
@@ -606,7 +642,7 @@
             collective_id=0, has_side_effects=True, vmem_limit_bytes=60 * 1024 * 1024
         ),
     )(field, cotangent, spectral_weight, point_weight, channel_bias.reshape(1, CH), *consts)
-    return layer, fgrad, wgrad
+    return store(layer, fgrad, wgrad)
 
 
 def solution(mesh):

time: 95.3 us -> 91.5 us (0.960)
  local copies, waits for them, and re-layouts: 4.25 us -> 0 us
    unnamed x7 -> x0, local copies, waits for them, and re-layouts: 4.25 us -> none
    pallas_call x0 -> x1, Pallas kernels: none -> 2.75 us  [store(): pl.pallas_call(store_kernel, out_shape=tuple((jax.ShapeDtypeStruct(a.shap...]
    pallas_call x1, Pallas kernels: 90.2 us -> 87.7 us  [per_device(): pl.pallas_call(kernel, out_shape=(jax.ShapeDtypeStruct(field.shape, BF),...]
where the time goes in v4:
time: 91.5 us; the launch traced here: 91.3 us
  Pallas kernels  90.5 us (99%)
    pallas_call x1, Pallas kernels, per_device(): pl.pallas_call(kernel, out_shape=(jax.ShapeDtypeStruct(field.shape, BF),...  87.7 us
    pallas_call x1, Pallas kernels, store(): pl.pallas_call(store_kernel, out_shape=tuple((jax.ShapeDtypeStruct(a.shap...  2.75 us

profile of v4, /device:TPU:1, one launch (start us, length us, event | category | flops | bytes accessed | tf_op | source)
XLA Modules:
  0.0 91.3 jit_solution(4318216164322692615)
XLA Ops:
  0.6 87.7 %shard_map.148 = (bf16[20,2,4,2048]{3,2,1,0:T(4,128)(2,1)}, bf16[20,2,4,2048]{3,2,1,0:T(4,128)(2,1)}, f32[36,7200]{1,0:T(8,128)}) custom-call(bf16[20,2,4,2048]{3,2,1,0:T(4,128)(2,1)} %field_hbm.1, bf16[20,2,4,2048]{3,2,1,0:T(4,128)(2,1)} %cot_hbm.1, bf16[36,7200]{1,0:T(8,128)(2,1)} %weight_hbm.1, bf16[20,20]{1,0:T(8,128)(2,1)} %point_ref.1, ...), custom_call_target="tpu_custom_call" | custom-call | tf_op jit(solution)/shard_map/pallas_call | solution.py:631
  88.4 2.8 %shard_map.149 = (bf16[20,2,4,2048]{3,2,1,0:T(4,128)(2,1)}, bf16[20,2,4,2048]{3,2,1,0:T(4,128)(2,1)}, f32[36,7200]{1,0:T(8,128)}) custom-call(bf16[20,2,4,2048]{3,2,1,0:T(4,128)(2,1)} %get-tuple-element.6.refs_0_, bf16[20,2,4,2048]{3,2,1,0:T(4,128)(2,1)} %get-tuple-element.7.refs_1_, f32[36,7200]{1,0:T(8,128)} %get-tuple-element.8.refs_2_), custom_call_target="tpu_custom_call" | custom-call | tf_op jit(solution)/shard_map/pallas_call | solution.py:571
